TPU v7x, 32 devices: a whole 2x2x4 slice. The times are simulated.
32 devices in a mesh: dp: 2 (over x), row: 2 (over core), col: 8 (over z, y).
Axes of the slice: x: 2, y: 2, z: 4, core: 2. Of those that a mesh axis runs over, the one named last changes fastest.
Arguments:
- features: bfloat16 [2, 48, 192, 256], P('dp', 'row', 'col'), may hold values from -8.5 to 8.5
- cotangent: bfloat16 [2, 48, 192, 256], P('dp', 'row', 'col'), may hold values from -4.5 to 4.5
- w_one: bfloat16 [256, 256], replicated, may hold values from -0.375 to 0.375
- w_point: bfloat16 [3, 256, 256], replicated, may hold values from -0.375 to 0.375
- taps: float32 [3, 3, 3, 256], replicated, may hold values from -2 to 2
- w_pool: bfloat16 [256, 256], replicated, may hold values from -0.375 to 0.375
- w_proj: bfloat16 [1280, 256], replicated, may hold values from -0.15625 to 0.15625
Outputs:
- mixed: bfloat16 [2, 48, 192, 256], P('dp', 'row', 'col')
- grad_input: bfloat16 [2, 48, 192, 256], P('dp', 'row', 'col')
- grad_one: float32 [256, 256], replicated
- grad_point: float32 [3, 256, 256], replicated
- grad_taps: float32 [3, 3, 3, 256], replicated
- grad_pool: float32 [256, 256], replicated
- grad_proj: float32 [1280, 256], replicated
All inputs are finite; a program needn't handle non-finite values.
Results may differ from a plain program's by a relative error of at most 0.0079.
Values may be sent and summed in bfloat16 or wider, within the bound.
A program may use at most 64 MiB of HBM per device.

v0:
```python
import math

import jax
import jax.numpy as jnp
from jax import lax
from jax.sharding import PartitionSpec as P

dilations = (6, 12, 18)
margin = 18


def with_halo(x, sides, width):
    for axis, dim in sides:
        devices, length = (lax.axis_size(axis), x.shape[dim])
        up = [(i, (i + 1) % devices) for i in range(devices - 1)]
        down = [(j, i) for i, j in up]
        last = lax.slice_in_dim(x, length - width, length, axis=dim)
        leading = lax.slice_in_dim(x, 0, width, axis=dim)
        before = lax.ppermute(last, axis, up)
        after = lax.ppermute(leading, axis, down)
        x = jnp.concatenate([before, x, after], axis=dim)
    return x


def silu_parts(value):
    sig = jax.nn.sigmoid(value)
    return (value * sig, sig * (1.0 + value * (1.0 - sig)))


def depthwise(padded, weights, rate, rows, cols, depth, offset_sign):
    total = None
    for i in range(3):
        for j in range(3):
            top = depth + offset_sign * rate * (i - 1)
            left = depth + offset_sign * rate * (j - 1)
            window = padded[:, top : top + rows, left : left + cols, :]
            piece = window.astype(jnp.float32) * weights[i, j]
            total = piece if total is None else total + piece
    return total


def tap_grads(padded, grad_depth, rate, rows, cols):
    stacked = []
    for i in range(3):
        line = []
        for j in range(3):
            top = margin + rate * (i - 1)
            left = margin + rate * (j - 1)
            window = padded[:, top : top + rows, left : left + cols, :]
            line.append(
                jnp.einsum("bhwc,bhwc->c", window, grad_depth, preferred_element_type=jnp.float32)
            )
        stacked.append(jnp.stack(line))
    return jnp.stack(stacked)


def contract_rows(left_mat, right_mat):
    return lax.dot_general(
        left_mat, right_mat, (((0,), (0,)), ((), ())), preferred_element_type=jnp.float32
    )


def contract_cols(left_mat, right_mat):
    return lax.dot_general(
        left_mat, right_mat, (((1,), (1,)), ((), ())), preferred_element_type=jnp.float32
    )


def shards(features, cotangent, w_one, w_point, taps, w_pool, w_proj):
    highest = lax.Precision.HIGHEST
    batch, rows, cols, in_chans = features.shape
    width = w_one.shape[1]
    count = batch * rows * cols
    image_cells = rows * cols * lax.axis_size("row") * lax.axis_size("col")
    scale = 1.0 / math.sqrt(image_cells * batch * lax.axis_size("dp"))
    main = w_proj[: 4 * width]
    last = w_proj[4 * width :].astype(jnp.float32)
    pool32 = w_pool.astype(jnp.float32)
    padded = with_halo(features, (("row", 1), ("col", 2)), margin)
    local_sum = jnp.sum(features, axis=(1, 2), dtype=jnp.float32)
    total_sum = lax.psum(local_sum, ("row", "col"))
    flat = features.reshape(count, in_chans)
    u_zero = jnp.dot(flat, w_one, preferred_element_type=jnp.float32)
    act, slope = silu_parts(u_zero)
    acts = [act.astype(jnp.bfloat16)]
    slopes = [slope]
    inner = []
    for k in range(3):
        depth_out = (
            depthwise(padded, taps[k], dilations[k], rows, cols, margin, 1)
            .astype(jnp.bfloat16)
            .reshape(count, in_chans)
        )
        u_k = jnp.dot(depth_out, w_point[k], preferred_element_type=jnp.float32)
        act, slope = silu_parts(u_k)
        acts.append(act.astype(jnp.bfloat16))
        slopes.append(slope)
        inner.append(depth_out)
    pooled = total_sum / image_cells
    q_val = jnp.dot(pooled, pool32, precision=highest)
    a_four, s_four = silu_parts(q_val)
    joined = jnp.concatenate(acts, axis=1)
    pre = jnp.dot(joined, main, preferred_element_type=jnp.float32).reshape(
        batch, rows * cols, width
    )
    pre = pre + jnp.dot(a_four, last, precision=highest)[:, None, :]
    mixed, s_pre = silu_parts(pre)
    mixed = mixed.astype(jnp.bfloat16).reshape(batch, rows, cols, width)
    dpre = (cotangent.reshape(batch, rows * cols, width).astype(jnp.float32) * s_pre).astype(
        jnp.bfloat16
    )
    slope_local = jnp.sum(dpre, axis=1, dtype=jnp.float32)
    dpre_flat = dpre.reshape(count, width)
    grad_main = contract_rows(joined, dpre_flat)
    owner = jnp.where((lax.axis_index("row") == 0) & (lax.axis_index("col") == 0), 1.0, 0.0).astype(
        jnp.float32
    )
    place = lax.axis_index("dp") * batch
    holder = jnp.zeros((batch * lax.axis_size("dp"), width), jnp.float32)
    holder = lax.dynamic_update_slice(holder, slope_local, (place, 0))
    grad_main, summed_holder = lax.psum((grad_main, holder), ("dp", "row", "col"))
    slope_total = lax.dynamic_slice(summed_holder, (place, 0), (batch, width))
    dcat = contract_cols(dpre_flat, main)
    dus = [
        (dcat[:, m * width : (m + 1) * width] * slopes[m]).astype(jnp.bfloat16) for m in range(4)
    ]
    grad_one = contract_rows(flat, dus[0])
    grad_point = jnp.stack([contract_rows(inner[k], dus[k + 1]) for k in range(3)])
    dq = jnp.dot(slope_total, last.T, precision=highest) * s_four
    dpooled = jnp.dot(dq, pool32.T, precision=highest)
    grad_pool = owner * lax.dot_general(pooled, dq, (((0,), (0,)), ((), ())), precision=highest)
    grad_four = owner * lax.dot_general(
        a_four, slope_total, (((0,), (0,)), ((), ())), precision=highest
    )
    grad_depths = [
        contract_cols(dus[k + 1], w_point[k])
        .astype(jnp.bfloat16)
        .reshape(batch, rows, cols, in_chans)
        for k in range(3)
    ]
    dx = contract_cols(dus[0], w_one).reshape(batch, rows, cols, in_chans)
    for k in range(3):
        rate = dilations[k]
        grad_pad = with_halo(grad_depths[k], (("row", 1), ("col", 2)), rate)
        dx = dx + depthwise(grad_pad, taps[k], rate, rows, cols, rate, -1)
    grad_taps = jnp.stack(
        [tap_grads(padded, grad_depths[k], dilations[k], rows, cols) for k in range(3)]
    )
    dx = dx + (dpooled / image_cells)[:, None, None, :]
    grad_input = dx.astype(jnp.bfloat16)
    grad_one, grad_point, grad_taps, grad_pool, grad_four = lax.psum(
        (grad_one, grad_point, grad_taps, grad_pool, grad_four), ("dp", "row", "col")
    )
    grad_proj = jnp.concatenate([grad_main, grad_four], axis=0)
    return (
        mixed,
        grad_input,
        grad_one * scale,
        grad_point * scale,
        grad_taps * scale,
        grad_pool * scale,
        grad_proj * scale,
    )


def solution(mesh):
    placed = (P("dp", "row", "col", None), P("dp", "row", "col", None), P(), P(), P(), P(), P())
    return jax.shard_map(
        shards,
        mesh=mesh,
        in_specs=placed,
        out_specs=(
            P("dp", "row", "col", None),
            P("dp", "row", "col", None),
            P(),
            P(),
            P(),
            P(),
            P(),
        ),
        check_vma=False,
    )
```

profile of v0, /device:TPU:0, one launch (start us, length us, event | category | flops | bytes accessed | tf_op | source)
XLA Modules:
  0.0 314.9 jit_solution(5095893078565390498)
XLA Ops:
  8.4 2.4 collective-permute-start
  10.8 1.3 collective-permute-start.1
  12.9 1.2 collective-permute-done.1
  15.5 5.1 %collective-permute-start.2 = (bf16[1,60,18,256]{3,1,2,0:T(8,128)(2,1)}, bf16[1,60,18,256]{3,1,2,0:T(8,128)(2,1)}, u32[]{:S(2)}, u32[]{:S(2)}) collective-permute-start(bf16[1,60,18,256]{3,1,2,0:T(8,128)(2,1)} %copy.46), channel_id=1, source_target_pairs={{0,1},{1,2},{2,3},{3,4},{4,5},{5,6},{6,7},{8,9},{9,10},{10,11},{11... | collective-permute-start | bytes 1658888 | tf_op jit(solution)/shard_map/ppermute | solution.py:19
  21.6 1.3 collective-permute-start.3
  24.8 21.0 %collective-permute-done.2 = bf16[1,60,18,256]{3,1,2,0:T(8,128)(2,1)} collective-permute-done((bf16[1,60,18,256]{3,1,2,0:T(8,128)(2,1)}, bf16[1,60,18,256]{3,1,2,0:T(8,128)(2,1)}, u32[]{:S(2)}, u32[]{:S(2)}) %collective-permute-start.2) | collective-permute-done | bytes 552992 | tf_op jit(solution)/shard_map/ppermute | solution.py:19
  45.8 1.4 copy.47
  47.1 1.4 copy.49
  48.6 1.5 fusion.5
  50.1 32.8 %psum.56 = f32[1,256]{1,0:T(1,128)S(1)} all-reduce(f32[1,256]{1,0:T(1,128)} %bitcast.446), channel_id=1, replica_groups=mesh['dp'=2,'row'=2,'col'=8] {'row','col'}, use_global_device_ids=true, to_apply=%region_1.0 | all-reduce | flops 256 | bytes 2048 | tf_op jit(solution)/shard_map/psum | solution.py:81
  84.0 1.3 multiply_convert_fusion.3
  89.1 1.9 convert_reduce_fusion.1
  91.1 1.6 fusion.69
  101.6 37.8 %all-reduce = (f32[2,256]{1,0:T(2,128)S(1)}, f32[3,3,3,256]{3,2,1,0:T(4,128)S(1)}) all-reduce(f32[2,256]{1,0:T(2,128)S(1)} %dynamic_update_slice.3, f32[3,3,3,256]{3,2,1,0:T(4,128)S(1)} %pad_maximum_fusion.30), channel_id=1, replica_groups=mesh['dp'=2,'row'=2,'col'=8] {'dp','row','col'}, use_global_device_ids=true, to_apply=%region_3.4 | all-reduce | flops 7424 | bytes 59392 | tf_op jit(solution)/shard_map/psum | solution.py:121
  142.5 1.3 collective-permute-start.4
  143.8 1.3 collective-permute-start.5
  145.1 3.0 collective-permute-start.8
  148.2 1.3 collective-permute-start.9
  149.5 3.0 collective-permute-start.12
  154.2 1.3 collective-permute-start.13
  155.5 1.3 collective-permute-start.6
  156.9 5.0 %collective-permute-start.7 = (bf16[1,36,6,256]{3,2,1,0:T(8,128)(2,1)S(1)}, bf16[1,36,6,256]{3,2,1,0:T(8,128)(2,1)S(1)}, u32[]{:S(2)}, u32[]{:S(2)}) collective-permute-start(bf16[1,36,6,256]{3,2,1,0:T(8,128)(2,1)S(1)} %get-tuple-element.94), channel_id=1, source_target_pairs={{0,1},{1,2},{2,3},{3,4},{4,5},{5,6},{6,7},{8,9},{9,10},{10,11},{11... | collective-permute-start | bytes 331784 | tf_op jit(solution)/shard_map/ppermute | solution.py:19
  163.3 1.3 collective-permute-start.14
  164.8 5.5 %collective-permute-start.15 = (bf16[1,60,18,256]{3,1,2,0:T(8,128)(2,1)S(1)}, bf16[1,60,18,256]{3,1,2,0:T(8,128)(2,1)S(1)}, u32[]{:S(2)}, u32[]{:S(2)}) collective-permute-start(bf16[1,60,18,256]{3,1,2,0:T(8,128)(2,1)S(1)} %copy.52), channel_id=1, source_target_pairs={{0,1},{1,2},{2,3},{3,4},{4,5},{5,6},{6,7},{8,9},{9,10},{10,11},{11... | collective-permute-start | bytes 1658888 | tf_op jit(solution)/shard_map/ppermute | solution.py:19
  170.4 1.3 collective-permute-start.10
  171.7 5.4 %collective-permute-start.11 = (bf16[1,48,12,256]{3,2,1,0:T(8,128)(2,1)S(1)}, bf16[1,48,12,256]{3,2,1,0:T(8,128)(2,1)S(1)}, u32[]{:S(2)}, u32[]{:S(2)}) collective-permute-start(bf16[1,48,12,256]{3,2,1,0:T(8,128)(2,1)S(1)} %get-tuple-element.89), channel_id=1, source_target_pairs={{0,1},{1,2},{2,3},{3,4},{4,5},{5,6},{6,7},{8,9},{9,10},{10,11},{11... | collective-permute-start | bytes 884744 | tf_op jit(solution)/shard_map/ppermute | solution.py:19
  177.8 6.2 %collective-permute-done.14 = bf16[1,60,18,256]{3,1,2,0:T(8,128)(2,1)S(1)} collective-permute-done((bf16[1,60,18,256]{3,1,2,0:T(8,128)(2,1)S(1)}, bf16[1,60,18,256]{3,1,2,0:T(8,128)(2,1)S(1)}, u32[]{:S(2)}, u32[]{:S(2)}) %collective-permute-start.14) | collective-permute-done | bytes 552992 | tf_op jit(solution)/shard_map/ppermute | solution.py:20
  184.3 23.4 %collective-permute-done.15 = bf16[1,60,18,256]{3,1,2,0:T(8,128)(2,1)S(1)} collective-permute-done((bf16[1,60,18,256]{3,1,2,0:T(8,128)(2,1)S(1)}, bf16[1,60,18,256]{3,1,2,0:T(8,128)(2,1)S(1)}, u32[]{:S(2)}, u32[]{:S(2)}) %collective-permute-start.15) | collective-permute-done | bytes 552992 | tf_op jit(solution)/shard_map/ppermute | solution.py:19
  208.1 8.1 %collective-permute-done.11 = bf16[1,48,12,256]{3,2,1,0:T(8,128)(2,1)S(1)} collective-permute-done((bf16[1,48,12,256]{3,2,1,0:T(8,128)(2,1)S(1)}, bf16[1,48,12,256]{3,2,1,0:T(8,128)(2,1)S(1)}, u32[]{:S(2)}, u32[]{:S(2)}) %collective-permute-start.11) | collective-permute-done | bytes 294944 | tf_op jit(solution)/shard_map/ppermute | solution.py:19
  216.4 3.9 %add_convert_fusion = bf16[1,24,24,256]{3,2,1,0:T(8,128)(2,1)} fusion(bf16[1,24,24,256]{3,2,1,0:T(8,128)(2,1)S(1)} %bitcast.343, bf16[1,24,24,256]{3,2,1,0:T(8,128)(2,1)S(1)} %bitcast.349, f32[1,24,24,256]{3,2,1,0:T(8,128)S(1)} %bitcast.350, bf16[1,24,24,256]{3,2,1,0:T(8,128)(2,1)S(1)} %bitcast.337, bf16[1,60,18,256]{3,2,1,0:T(8,128)(2,1)S(1)} %copy.53, ...), kind=kLoop, calls=%fused_computation.133 | loop fusion | flops 27279360 | bytes 6148096 | tf_op jit(solution)/shard_map/convert_element_type | solution.py:150
  220.3 81.5 %all-reduce.4.cloned.1.call-done = (f32[256,256]{0,1:T(8,128)}, f32[3,256,256]{2,1,0:T(8,128)}, f32[256,256]{0,1:T(8,128)}, f32[256,256]{0,1:T(8,128)}, f32[1024,256]{1,0:T(8,128)}) async-done(((f32[256,256]{0,1:T(8,128)}, f32[3,256,256]{2,1,0:T(8,128)}, f32[256,256]{0,1:T(8,128)}, f32[256,256]{0,1:T(8,128)}, f32[1024,256]{1,0:T(8,128)}), (f32[256,256]{0,1:T(8,128)}, f32[3,256,256]{2,1,0:T(8,128)}, ...) | async-done | bytes 2621456 | tf_op jit(solution)/shard_map/psum | solution.py:151
  303.0 2.2 broadcast_multiply_fusion
  (236 shorter events, 31.2 us)
Async XLA Ops:
  7.2 294.6 %all-reduce.4.cloned.1.call-start = ((), (), s32[]{:S(2)}) async-start(), calls=%async_computation | async-start | bytes 5242880 | tf_op jit(solution)/shard_map/psum | solution.py:151
  8.4 4.4 %collective-permute-start = (bf16[1,18,24,256]{3,2,1,0:T(8,128)(2,1)S(1)}, bf16[1,18,24,256]{3,2,1,0:T(8,128)(2,1)S(1)}, u32[]{:S(2)}, u32[]{:S(2)}) collective-permute-start(bf16[1,18,24,256]{3,2,1,0:T(8,128)(2,1)S(1)} %get-tuple-element.106), channel_id=1, source_target_pairs={{0,8},{1,9},{2,10},{3,11},{4,12},{5,13},{6,14},{7,15},{16,24},{17,... | collective-permute-start | bytes 663560 | tf_op jit(solution)/shard_map/ppermute | solution.py:19
  10.8 3.4 %collective-permute-start.1 = (bf16[1,18,24,256]{3,2,1,0:T(8,128)(2,1)S(1)}, bf16[1,18,24,256]{3,2,1,0:T(8,128)(2,1)S(1)}, u32[]{:S(2)}, u32[]{:S(2)}) collective-permute-start(bf16[1,18,24,256]{3,2,1,0:T(8,128)(2,1)S(1)} %get-tuple-element.107), channel_id=1, source_target_pairs={{8,0},{9,1},{10,2},{11,3},{12,4},{13,5},{14,6},{15,7},{24,16},{25,... | collective-permute-start | bytes 663560 | tf_op jit(solution)/shard_map/ppermute | solution.py:20
  14.2 72.8 %copy-start.2 = (bf16[1,42,24,256]{3,2,1,0:T(8,128)(2,1)}, bf16[1,42,24,256]{3,2,1,0:T(8,128)(2,1)S(1)}, u32[]{:S(2)}) copy-start(bf16[1,42,24,256]{3,2,1,0:T(8,128)(2,1)S(1)} %get-tuple-element.109) | copy-start | bytes 1548292
  15.5 30.2 %collective-permute-start.2 = (bf16[1,60,18,256]{3,1,2,0:T(8,128)(2,1)}, bf16[1,60,18,256]{3,1,2,0:T(8,128)(2,1)}, u32[]{:S(2)}, u32[]{:S(2)}) collective-permute-start(bf16[1,60,18,256]{3,1,2,0:T(8,128)(2,1)} %copy.46), channel_id=1, source_target_pairs={{0,1},{1,2},{2,3},{3,4},{4,5},{5,6},{6,7},{8,9},{9,10},{10,11},{11... | collective-permute-start | bytes 1658888 | tf_op jit(solution)/shard_map/ppermute | solution.py:19
  21.6 25.6 %collective-permute-start.3 = (bf16[1,60,18,256]{3,1,2,0:T(8,128)(2,1)}, bf16[1,60,18,256]{3,1,2,0:T(8,128)(2,1)}, u32[]{:S(2)}, u32[]{:S(2)}) collective-permute-start(bf16[1,60,18,256]{3,1,2,0:T(8,128)(2,1)} %copy.48), channel_id=1, source_target_pairs={{1,0},{2,1},{3,2},{4,3},{5,4},{6,5},{7,6},{9,8},{10,9},{11,10},{12... | collective-permute-start | bytes 1658888 | tf_op jit(solution)/shard_map/ppermute | solution.py:20
  22.9 64.1 %copy-start.27 = (f32[1,1,256]{2,1,0:T(1,128)}, f32[1,1,256]{2,1,0:T(1,128)S(1)}, u32[]{:S(2)}) copy-start(f32[1,1,256]{2,1,0:T(1,128)S(1)} %get-tuple-element.141) | copy-start | bytes 3076
  23.6 61.8 %copy-start.47 = (f32[1,1,256]{2,1,0:T(1,128)}, f32[1,1,256]{2,1,0:T(1,128)S(1)}, u32[]{:S(2)}) copy-start(f32[1,1,256]{2,1,0:T(1,128)S(1)} %get-tuple-element.150) | copy-start | bytes 3076
  23.6 61.8 %copy-start.49 = (f32[1,1,256]{2,1,0:T(1,128)}, f32[1,1,256]{2,1,0:T(1,128)S(1)}, u32[]{:S(2)}) copy-start(f32[1,1,256]{2,1,0:T(1,128)S(1)} %get-tuple-element.151) | copy-start | bytes 3076
  23.6 61.8 %copy-start.51 = (f32[1,1,256]{2,1,0:T(1,128)}, f32[1,1,256]{2,1,0:T(1,128)S(1)}, u32[]{:S(2)}) copy-start(f32[1,1,256]{2,1,0:T(1,128)S(1)} %get-tuple-element.152) | copy-start | bytes 3076
  23.6 61.8 %copy-start.53 = (f32[1,1,256]{2,1,0:T(1,128)}, f32[1,1,256]{2,1,0:T(1,128)S(1)}, u32[]{:S(2)}) copy-start(f32[1,1,256]{2,1,0:T(1,128)S(1)} %get-tuple-element.153) | copy-start | bytes 3076
  23.6 61.8 %copy-start.55 = (f32[1,1,256]{2,1,0:T(1,128)}, f32[1,1,256]{2,1,0:T(1,128)S(1)}, u32[]{:S(2)}) copy-start(f32[1,1,256]{2,1,0:T(1,128)S(1)} %get-tuple-element.154) | copy-start | bytes 3076
  23.6 61.8 %copy-start.57 = (f32[1,1,256]{2,1,0:T(1,128)}, f32[1,1,256]{2,1,0:T(1,128)S(1)}, u32[]{:S(2)}) copy-start(f32[1,1,256]{2,1,0:T(1,128)S(1)} %get-tuple-element.155) | copy-start | bytes 3076
  23.6 61.8 %copy-start.59 = (f32[1,1,256]{2,1,0:T(1,128)}, f32[1,1,256]{2,1,0:T(1,128)S(1)}, u32[]{:S(2)}) copy-start(f32[1,1,256]{2,1,0:T(1,128)S(1)} %get-tuple-element.156) | copy-start | bytes 3076
  23.6 61.8 %copy-start.61 = (f32[1,1,256]{2,1,0:T(1,128)}, f32[1,1,256]{2,1,0:T(1,128)S(1)}, u32[]{:S(2)}) copy-start(f32[1,1,256]{2,1,0:T(1,128)S(1)} %get-tuple-element.157) | copy-start | bytes 3076
  100.6 39.9 %copy-start.68 = (f32[1,256]{1,0:T(1,128)S(1)}, f32[1,256]{1,0:T(1,128)}, u32[]{:S(2)}) copy-start(f32[1,256]{1,0:T(1,128)} %copy-done.67) | copy-start | bytes 3076
  100.6 40.0 %copy-start.66 = (f32[256]{0:T(256)S(1)}, f32[256]{0:T(256)}, u32[]{:S(2)}) copy-start(f32[256]{0:T(256)} %copy-done.65) | copy-start | bytes 3076
  100.6 41.6 %copy-start.23 = (bf16[256,256]{1,0:T(8,128)(2,1)S(1)}, bf16[256,256]{1,0:T(8,128)(2,1)}, u32[]{:S(2)}) copy-start(bf16[256,256]{1,0:T(8,128)(2,1)} %param.12) | copy-start | bytes 393220
  142.5 11.7 %collective-permute-start.4 = (bf16[1,6,24,256]{3,2,1,0:T(8,128)(2,1)S(1)}, bf16[1,6,24,256]{3,2,1,0:T(8,128)(2,1)S(1)}, u32[]{:S(2)}, u32[]{:S(2)}) collective-permute-start(bf16[1,6,24,256]{3,2,1,0:T(8,128)(2,1)S(1)} %get-tuple-element.95), channel_id=1, source_target_pairs={{0,8},{1,9},{2,10},{3,11},{4,12},{5,13},{6,14},{7,15},{16,24},{17,... | collective-permute-start | bytes 221192 | tf_op jit(solution)/shard_map/ppermute | solution.py:19
  143.8 11.7 %collective-permute-start.5 = (bf16[1,6,24,256]{3,2,1,0:T(8,128)(2,1)S(1)}, bf16[1,6,24,256]{3,2,1,0:T(8,128)(2,1)S(1)}, u32[]{:S(2)}, u32[]{:S(2)}) collective-permute-start(bf16[1,6,24,256]{3,2,1,0:T(8,128)(2,1)S(1)} %get-tuple-element.96), channel_id=1, source_target_pairs={{8,0},{9,1},{10,2},{11,3},{12,4},{13,5},{14,6},{15,7},{24,16},{25,... | collective-permute-start | bytes 221192 | tf_op jit(solution)/shard_map/ppermute | solution.py:20
  145.1 11.7 %collective-permute-start.8 = (bf16[1,12,24,256]{3,2,1,0:T(8,128)(2,1)S(1)}, bf16[1,12,24,256]{3,2,1,0:T(8,128)(2,1)S(1)}, u32[]{:S(2)}, u32[]{:S(2)}) collective-permute-start(bf16[1,12,24,256]{3,2,1,0:T(8,128)(2,1)S(1)} %get-tuple-element.97), channel_id=1, source_target_pairs={{0,8},{1,9},{2,10},{3,11},{4,12},{5,13},{6,14},{7,15},{16,24},{17,... | collective-permute-start | bytes 442376 | tf_op jit(solution)/shard_map/ppermute | solution.py:19
  148.2 13.7 %collective-permute-start.9 = (bf16[1,12,24,256]{3,2,1,0:T(8,128)(2,1)S(1)}, bf16[1,12,24,256]{3,2,1,0:T(8,128)(2,1)S(1)}, u32[]{:S(2)}, u32[]{:S(2)}) collective-permute-start(bf16[1,12,24,256]{3,2,1,0:T(8,128)(2,1)S(1)} %get-tuple-element.98), channel_id=1, source_target_pairs={{8,0},{9,1},{10,2},{11,3},{12,4},{13,5},{14,6},{15,7},{24,16},{25,... | collective-permute-start | bytes 442376 | tf_op jit(solution)/shard_map/ppermute | solution.py:20
  149.5 12.5 %collective-permute-start.12 = (bf16[1,18,24,256]{3,2,1,0:T(8,128)(2,1)S(1)}, bf16[1,18,24,256]{3,2,1,0:T(8,128)(2,1)S(1)}, u32[]{:S(2)}, u32[]{:S(2)}) collective-permute-start(bf16[1,18,24,256]{3,2,1,0:T(8,128)(2,1)S(1)} %get-tuple-element.99), channel_id=1, source_target_pairs={{0,8},{1,9},{2,10},{3,11},{4,12},{5,13},{6,14},{7,15},{16,24},{17,... | collective-permute-start | bytes 663560 | tf_op jit(solution)/shard_map/ppermute | solution.py:19
  154.2 7.9 %collective-permute-start.13 = (bf16[1,18,24,256]{3,2,1,0:T(8,128)(2,1)S(1)}, bf16[1,18,24,256]{3,2,1,0:T(8,128)(2,1)S(1)}, u32[]{:S(2)}, u32[]{:S(2)}) collective-permute-start(bf16[1,18,24,256]{3,2,1,0:T(8,128)(2,1)S(1)} %get-tuple-element.100), channel_id=1, source_target_pairs={{8,0},{9,1},{10,2},{11,3},{12,4},{13,5},{14,6},{15,7},{24,16},{25,... | collective-permute-start | bytes 663560 | tf_op jit(solution)/shard_map/ppermute | solution.py:20
  155.5 16.2 %collective-permute-start.6 = (bf16[1,36,6,256]{3,2,1,0:T(8,128)(2,1)S(1)}, bf16[1,36,6,256]{3,2,1,0:T(8,128)(2,1)S(1)}, u32[]{:S(2)}, u32[]{:S(2)}) collective-permute-start(bf16[1,36,6,256]{3,2,1,0:T(8,128)(2,1)S(1)} %get-tuple-element.93), channel_id=1, source_target_pairs={{1,0},{2,1},{3,2},{4,3},{5,4},{6,5},{7,6},{9,8},{10,9},{11,10},{12... | collective-permute-start | bytes 331784 | tf_op jit(solution)/shard_map/ppermute | solution.py:20
  156.9 20.3 %collective-permute-start.7 = (bf16[1,36,6,256]{3,2,1,0:T(8,128)(2,1)S(1)}, bf16[1,36,6,256]{3,2,1,0:T(8,128)(2,1)S(1)}, u32[]{:S(2)}, u32[]{:S(2)}) collective-permute-start(bf16[1,36,6,256]{3,2,1,0:T(8,128)(2,1)S(1)} %get-tuple-element.94), channel_id=1, source_target_pairs={{0,1},{1,2},{2,3},{3,4},{4,5},{5,6},{6,7},{8,9},{9,10},{10,11},{11... | collective-permute-start | bytes 331784 | tf_op jit(solution)/shard_map/ppermute | solution.py:19
  163.3 20.7 %collective-permute-start.14 = (bf16[1,60,18,256]{3,1,2,0:T(8,128)(2,1)S(1)}, bf16[1,60,18,256]{3,1,2,0:T(8,128)(2,1)S(1)}, u32[]{:S(2)}, u32[]{:S(2)}) collective-permute-start(bf16[1,60,18,256]{3,1,2,0:T(8,128)(2,1)S(1)} %copy.50), channel_id=1, source_target_pairs={{1,0},{2,1},{3,2},{4,3},{5,4},{6,5},{7,6},{9,8},{10,9},{11,10},{12... | collective-permute-start | bytes 1658888 | tf_op jit(solution)/shard_map/ppermute | solution.py:20
  164.8 43.0 %collective-permute-start.15 = (bf16[1,60,18,256]{3,1,2,0:T(8,128)(2,1)S(1)}, bf16[1,60,18,256]{3,1,2,0:T(8,128)(2,1)S(1)}, u32[]{:S(2)}, u32[]{:S(2)}) collective-permute-start(bf16[1,60,18,256]{3,1,2,0:T(8,128)(2,1)S(1)} %copy.52), channel_id=1, source_target_pairs={{0,1},{1,2},{2,3},{3,4},{4,5},{5,6},{6,7},{8,9},{9,10},{10,11},{11... | collective-permute-start | bytes 1658888 | tf_op jit(solution)/shard_map/ppermute | solution.py:19
  170.4 37.7 %collective-permute-start.10 = (bf16[1,48,12,256]{3,2,1,0:T(8,128)(2,1)S(1)}, bf16[1,48,12,256]{3,2,1,0:T(8,128)(2,1)S(1)}, u32[]{:S(2)}, u32[]{:S(2)}) collective-permute-start(bf16[1,48,12,256]{3,2,1,0:T(8,128)(2,1)S(1)} %get-tuple-element.88), channel_id=1, source_target_pairs={{1,0},{2,1},{3,2},{4,3},{5,4},{6,5},{7,6},{9,8},{10,9},{11,10},{12... | collective-permute-start | bytes 884744 | tf_op jit(solution)/shard_map/ppermute | solution.py:20
  171.7 44.5 %collective-permute-start.11 = (bf16[1,48,12,256]{3,2,1,0:T(8,128)(2,1)S(1)}, bf16[1,48,12,256]{3,2,1,0:T(8,128)(2,1)S(1)}, u32[]{:S(2)}, u32[]{:S(2)}) collective-permute-start(bf16[1,48,12,256]{3,2,1,0:T(8,128)(2,1)S(1)} %get-tuple-element.89), channel_id=1, source_target_pairs={{0,1},{1,2},{2,3},{3,4},{4,5},{5,6},{6,7},{8,9},{9,10},{10,11},{11... | collective-permute-start | bytes 884744 | tf_op jit(solution)/shard_map/ppermute | solution.py:19
  177.6 38.6 %copy-start.7 = (f32[576,256]{1,0:T(8,128)S(1)}, f32[576,256]{1,0:T(8,128)}, u32[]{:S(2)}) copy-start(f32[576,256]{1,0:T(8,128)} %fusion.106) | copy-start | bytes 1769476
  177.6 38.6 %copy-start.13 = (bf16[1,18,24,256]{3,2,1,0:T(8,128)(2,1)S(1)}, bf16[1,18,24,256]{3,2,1,0:T(8,128)(2,1)}, u32[]{:S(2)}) copy-start(bf16[1,18,24,256]{3,2,1,0:T(8,128)(2,1)} %copy-done.12) | copy-start | bytes 663556
  (59 other events, 1281.7 us)
Sparse Core Ops, SparseCore 0:
  154.3 147.4 all-reduce.3
where the time goes:
time: 316 us; the launch traced here: 315 us
  waiting for transfers between devices  141 us (45%)
  blocking collectives  70.6 us (22%)
  starting transfers between devices  41.2 us (13%)
  other arithmetic  18.6 us (6%)
  between operations  15.6 us (5%)
  local copies, waits for them, and re-layouts  14.3 us (5%)
  matrix products  13.3 us (4%)
    psum x1, waiting for transfers between devices, shards(): lax.psum((grad_one, grad_point, grad_taps, grad_pool, grad_four), ('dp',...  81.5 us
    ppermute x8, waiting for transfers between devices, with_halo(): before = lax.ppermute(last, axis, up)  52.5 us
    psum x1, blocking collectives, shards(): lax.psum((grad_main, holder), ('dp', 'row', 'col'))  37.8 us
    psum x1, blocking collectives, shards(): total_sum = lax.psum(local_sum, ('row', 'col'))  32.8 us
    ppermute x8, starting transfers between devices, with_halo(): before = lax.ppermute(last, axis, up)  30.8 us
    ppermute x8, starting transfers between devices, with_halo(): after = lax.ppermute(leading, axis, down)  10.3 us
    ppermute x8, waiting for transfers between devices, with_halo(): after = lax.ppermute(leading, axis, down)  7.37 us
  transfers between devices with their start and end apart: 17, of which 6 were waited for; matrix products, arithmetic and copies ran while one was open for 4% of the time, Pallas kernels for 0%

commit v1 on v0

v1 whole, which is shorter than its diff:
```python
import functools
import math

import jax
import jax.numpy as jnp
from jax import lax
from jax.experimental import pallas as pl
from jax.experimental.pallas import tpu as pltpu
from jax.sharding import PartitionSpec as P

unit = 6
margin = 18
reach = margin // unit
edge = 112
MESH = pl.DeviceIdType.MESH
f32 = jnp.float32
bf16 = jnp.bfloat16
highest = lax.Precision.HIGHEST


def silu_parts(value):
    sig = jax.nn.sigmoid(value)
    return value * sig, sig * (1.0 + value * (1.0 - sig))


def dot(a, b):
    return jnp.dot(a, b, preferred_element_type=f32)


def dot_nt(a, b):
    return lax.dot_general(a, b, (((1,), (1,)), ((), ())), preferred_element_type=f32)


def dot_tn(a, b):
    return lax.dot_general(a, b, (((0,), (0,)), ((), ())), preferred_element_type=f32)


def fold8(value):
    return jnp.sum(value.reshape(value.shape[0] // 8, 8, value.shape[1]), axis=0)


def kernel(
    n_dp, n_row, n_col, image_cells,
    x_in, cot, w_one, w_point, taps, w_pool, w_proj,
    mixed_out, dx_out, grads_out, taps_out, pool_out, four_out,
    xp, x32, part, slopes, acts, inner, pre_s, dpre_s, du_s, dz_s, dx0,
    slots, images, term, tapacc,
    g32, gb, g_ra, b1, g_rb, b2, g_rc, final,
    t_row, t_dp, t_col,
    row_send, row_recv, col_send, col_recv,
    sm_s, sm_r, xc_s, xc_r, xr_s, xr_r, pr_s, pr_r, pc_s, pc_r,
    ga_s, ga_r, gbs, gbr, gc_s, gc_r, ha_s, ha_r, hb_s, hb_r, hc_s, hc_r,
    ta_s, ta_r, tb_s, tb_r, tc_s, tc_r,
):
    d, r, c = lax.axis_index("dp"), lax.axis_index("row"), lax.axis_index("col")
    total = n_dp * n_row * n_col
    per = n_row * n_col
    me = (d * n_row + r) * n_col + c
    blocks, depth, ch = x_in.shape
    wide = blocks + 2 * reach
    lo, hi = edge, edge + depth

    def peer(i):
        p = lax.rem(me + i, total)
        return {
            "dp": lax.div(p, per),
            "row": lax.rem(lax.div(p, n_col), n_row),
            "col": lax.rem(p, n_col),
        }

    def remote(src, dst, ss, rs, dev):
        return pltpu.make_async_remote_copy(
            src_ref=src, dst_ref=dst, send_sem=ss, recv_sem=rs, device_id=dev, device_id_type=MESH
        )

    barrier = pltpu.get_barrier_semaphore()

    xp[...] = jnp.zeros_like(xp)
    ones = jnp.zeros((8, ch), f32)
    for a in range(blocks):
        block = x_in[a]
        xp[reach + a, lo:hi] = block
        ones = ones + fold8(block.astype(f32))
    slots[0, me] = ones

    @pl.loop(1, total)
    def _(i):
        pl.semaphore_signal(barrier, inc=1, device_id=peer(i), device_id_type=MESH)

    pl.semaphore_wait(barrier, total - 1)

    right, left = {"col": lax.rem(c + 1, n_col)}, {"col": lax.rem(c + n_col - 1, n_col)}
    below, above = {"row": lax.rem(r + 1, n_row)}, {"row": lax.rem(r + n_row - 1, n_row)}
    has_right, has_left = c < n_col - 1, c > 0
    has_below, has_above = r < n_row - 1, r > 0

    def col_copy(side):
        src, dst = (wide - 2 * reach, 0) if side == 0 else (reach, wide - reach)
        mid = pl.ds(lo, depth)
        return remote(
            xp.at[pl.ds(src, reach), mid], xp.at[pl.ds(dst, reach), mid],
            xc_s.at[side], xc_r.at[side], right if side == 0 else left,
        )

    def row_copy(side, seg):
        span = (pl.ds(reach, blocks), pl.ds(0, reach), pl.ds(wide - reach, reach))[seg]
        src, dst = (hi - edge, 0) if side == 0 else (lo, hi)
        return remote(
            xp.at[span, pl.ds(src, edge)], xp.at[span, pl.ds(dst, edge)],
            xr_s.at[side * 3 + seg], xr_r.at[side * 3 + seg], below if side == 0 else above,
        )

    sends = ((has_right, has_left), (has_left, has_right))
    row_sends = ((has_below, has_above), (has_above, has_below))
    for side in range(2):
        @pl.when(sends[side][0])
        def _():
            col_copy(side).start()
    for side in range(2):
        @pl.when(row_sends[side][0])
        def _():
            row_copy(side, 0).start()

    def small_start(which):
        @pl.loop(1, total)
        def _(i):
            remote(
                slots.at[which, me], slots.at[which, me], sm_s.at[which], sm_r.at[which], peer(i)
            ).start()

    def small_wait(which):
        rest = slots.at[which, pl.ds(0, total - 1)]
        remote(rest, rest, sm_s.at[which], sm_r.at[which], peer(1)).wait()

    def small_sums(which):
        images[which] = jnp.zeros((8, ch), f32)
        for b in range(n_dp):
            acc = jnp.sum(slots[which, b * per : (b + 1) * per], axis=0)
            images[which, b : b + 1] = jnp.sum(acc, axis=0, keepdims=True)
        return images[which]

    small_start(0)

    @pl.loop(0, blocks)
    def _(a):
        here = pl.ds(a * depth, depth)
        u = dot(x_in[a], w_one[...])
        act, slope = silu_parts(u)
        act = act.astype(bf16)
        acts[0, here] = act
        slopes[0, here] = slope
        pre_s[here] = dot(act, w_proj[0:ch])

    @pl.loop(0, wide)
    def _(a):
        part[a] = jnp.zeros(part.shape[1:], f32)

    tapacc[...] = jnp.zeros_like(tapacc)

    for side in range(2):
        @pl.when(sends[side][1])
        def _():
            col_copy(side).wait_recv()
            for rside in range(2):
                @pl.when(row_sends[rside][0])
                def _():
                    row_copy(rside, 1 + side).start()

    for side in range(2):
        @pl.when(row_sends[side][1])
        def _():
            row_copy(side, 0).wait_recv()
            for cside in range(2):
                @pl.when(sends[cside][1])
                def _():
                    row_copy(side, 1 + cside).wait_recv()

    @pl.loop(0, wide)
    def _(a):
        x32[a] = xp[a].astype(f32)

    @pl.loop(0, blocks)
    def _(a):
        here = pl.ds(a * depth, depth)
        pre = pre_s[here]
        for k in range(3):
            acc = None
            for i in range(3):
                for j in range(3):
                    row = lo + 36 * (k + 1) * (i - 1)
                    win = x32[a + reach + (k + 1) * (j - 1), row : row + depth]
                    piece = win * taps[k, i, j : j + 1, :]
                    acc = piece if acc is None else acc + piece
            z = acc.astype(bf16)
            inner[k, here] = z
            act, slope = silu_parts(dot(z, w_point[k]))
            act = act.astype(bf16)
            acts[k + 1, here] = act
            slopes[k + 1, here] = slope
            pre = pre + dot(act, w_proj[(k + 1) * ch : (k + 2) * ch])
        pre_s[here] = pre

    small_wait(0)
    pooled = small_sums(0) * (1.0 / image_cells)
    pool32 = w_pool[...].astype(f32)
    last = w_proj[4 * ch : 5 * ch].astype(f32)
    q = jnp.dot(pooled, pool32, precision=highest, preferred_element_type=f32)
    a_four, s_four = silu_parts(q)
    term[...] = jnp.dot(a_four, last, precision=highest, preferred_element_type=f32)
    own_term = term[pl.ds(d, 1), :]

    slots[1, me] = jnp.zeros((8, ch), f32)

    @pl.loop(0, blocks)
    def _(a):
        here = pl.ds(a * depth, depth)
        out, slope = silu_parts(pre_s[here] + own_term)
        mixed_out[a] = out.astype(bf16)
        dpre = (cot[a].astype(f32) * slope).astype(bf16)
        dpre_s[here] = dpre
        slots[1, me] += fold8(dpre.astype(f32))

    small_start(1)

    @pl.loop(0, blocks)
    def _(a):
        here = pl.ds(a * depth, depth)
        dpre = dpre_s[here]
        for m in range(4):
            dcat = dot_nt(dpre, w_proj[m * ch : (m + 1) * ch])
            du = (dcat * slopes[m, here]).astype(bf16)
            du_s[m, here] = du
            if m == 0:
                dx0[a] = dot_nt(du, w_one[...])
            else:
                dz_s[m - 1, here] = dot_nt(du, w_point[m - 1]).astype(bf16)

    for m in range(4):
        g = dot_tn(acts[m], dpre_s[...])
        g32[m * ch : (m + 1) * ch] = g
        gb[m * ch : (m + 1) * ch] = g.astype(bf16)
    for m in range(4):
        g = dot_tn(x_flat(x_in) if m == 0 else inner[m - 1], du_s[m])
        g32[(4 + m) * ch : (5 + m) * ch] = g
        gb[(4 + m) * ch : (5 + m) * ch] = g.astype(bf16)

    whole = g32.shape[0]
    per_row, per_dp, per_col = (
        whole // n_row,
        whole // (n_row * n_dp),
        whole // (n_row * n_dp * n_col),
    )

    def scatter(n, axis, at, size, src, dst, ss, rs):
        out = []
        for i in range(1, n):
            to = lax.rem(at + i, n)
            out.append(
                remote(
                    src.at[pl.ds(pl.multiple_of(to * size, 16), size)], dst.at[i - 1],
                    ss.at[i - 1], rs.at[i - 1], {axis: to},
                )
            )
        return out

    def gather(n, axis, at, base, size, ss, rs):
        own = final.at[pl.ds(pl.multiple_of(base + at * size, 16), size)]
        return [
            remote(own, own, ss.at[i - 1], rs.at[i - 1], {axis: lax.rem(at + i, n)})
            for i in range(1, n)
        ]

    def spread(n, axis, at, buf, ss, rs):
        return [
            remote(buf.at[at], buf.at[at], ss.at[i - 1], rs.at[i - 1], {axis: lax.rem(at + i, n)})
            for i in range(1, n)
        ]

    def start(copies):
        for copy in copies:
            copy.start()

    def wait(copies):
        for copy in copies:
            copy.wait()

    ga = scatter(n_row, "row", r, per_row, gb, g_ra, ga_s, ga_r)
    start(ga)

    @pl.loop(0, blocks)
    def _(a):
        here = pl.ds(a * depth, depth)
        for k in range(3):
            dz = dz_s[k, here].astype(f32)
            for i in range(3):
                for j in range(3):
                    row = lo + 36 * (k + 1) * (i - 1)
                    at = a + reach + (k + 1) * (j - 1)
                    tapacc[9 * k + 3 * i + j] += fold8(x32[at, row : row + depth] * dz)
                    part[at, row : row + depth] += dz * taps[k, i, j : j + 1, :]

    for side in range(2):
        @pl.when(row_sends[side][0])
        def _():
            src = hi if side == 0 else 0
            @pl.loop(0, wide)
            def _(a):
                row_send[side, a] = part[a, src : src + edge].astype(bf16)
            remote(
                row_send.at[side], row_recv.at[side], pr_s.at[side], pr_r.at[side],
                below if side == 0 else above,
            ).start()

    wait(ga)
    mine = pl.multiple_of(r * per_row, 16)
    for s in range(0, per_row, 128):
        acc = g32[pl.ds(pl.multiple_of(mine + s, 16), 128)]
        for i in range(n_row - 1):
            acc = acc + g_ra[i, s : s + 128].astype(f32)
        g32[pl.ds(pl.multiple_of(mine + s, 16), 128)] = acc
        b1[s : s + 128] = acc.astype(bf16)
    gbc = scatter(n_dp, "dp", d, per_dp, b1, g_rb, gbs, gbr)
    start(gbc)

    t_row[r] = jnp.zeros(t_row.shape[1:], f32)
    for t in range(27):
        t_row[r, t : t + 1] = jnp.sum(tapacc[t], axis=0, keepdims=True)
    ta = spread(n_row, "row", r, t_row, ta_s, ta_r)
    start(ta)

    for side in range(2):
        @pl.when(row_sends[side][1])
        def _():
            remote(
                row_send.at[side], row_recv.at[side], pr_s.at[side], pr_r.at[side],
                below if side == 0 else above,
            ).wait_recv()
            dst = lo if side == 0 else hi - edge
            @pl.loop(0, wide)
            def _(a):
                part[a, dst : dst + edge] += row_recv[side, a].astype(f32)

    def back_copy(side):
        return remote(
            col_send.at[side], col_recv.at[side], pc_s.at[side], pc_r.at[side],
            right if side == 0 else left,
        )

    for side in range(2):
        @pl.when(sends[side][0])
        def _():
            src = wide - reach if side == 0 else 0
            for a in range(reach):
                col_send[side, a] = part[src + a, lo:hi].astype(bf16)
            back_copy(side).start()

    wait(ta)
    t_dp[d] = jnp.sum(t_row[...], axis=0)
    tb = spread(n_dp, "dp", d, t_dp, tb_s, tb_r)
    start(tb)

    wait(gbc)
    mine = pl.multiple_of(mine + d * per_dp, 16)
    for s in range(0, per_dp, 64):
        acc = g32[pl.ds(pl.multiple_of(mine + s, 16), 64)]
        for i in range(n_dp - 1):
            acc = acc + g_rb[i, s : s + 64].astype(f32)
        g32[pl.ds(pl.multiple_of(mine + s, 16), 64)] = acc
        b2[s : s + 64] = acc.astype(bf16)
    gc = scatter(n_col, "col", c, per_col, b2, g_rc, gc_s, gc_r)
    start(gc)

    wait(tb)
    t_col[c] = jnp.sum(t_dp[...], axis=0)
    tc = spread(n_col, "col", c, t_col, tc_s, tc_r)
    start(tc)

    small_wait(1)
    slope_total = small_sums(1)
    dq = (
        lax.dot_general(
            slope_total, last, (((1,), (1,)), ((), ())), precision=highest,
            preferred_element_type=f32,
        )
        * s_four
    )
    dpooled = lax.dot_general(
        dq, pool32, (((1,), (1,)), ((), ())), precision=highest, preferred_element_type=f32
    )
    term[...] = dpooled * (1.0 / image_cells)
    own_mean = term[pl.ds(d, 1), :]
    scale = 1.0 / math.sqrt(image_cells * n_dp)
    pool_out[...] = scale * lax.dot_general(
        pooled, dq, (((0,), (0,)), ((), ())), precision=highest, preferred_element_type=f32
    )
    four_out[...] = scale * lax.dot_general(
        a_four, slope_total, (((0,), (0,)), ((), ())), precision=highest,
        preferred_element_type=f32,
    )

    wait(gc)
    mine = pl.multiple_of(mine + c * per_col, 16)
    acc = g32[pl.ds(mine, per_col)]
    for i in range(n_col - 1):
        acc = acc + g_rc[i].astype(f32)
    final[pl.ds(mine, per_col)] = acc.astype(bf16)
    hc = gather(n_col, "col", c, r * per_row + d * per_dp, per_col, hc_s, hc_r)
    start(hc)

    for side in range(2):
        @pl.when(sends[side][1])
        def _():
            back_copy(side).wait_recv()
            dst = reach if side == 0 else wide - 2 * reach
            for a in range(reach):
                part[dst + a, lo:hi] += col_recv[side, a].astype(f32)

    @pl.loop(0, blocks)
    def _(a):
        dx_out[a] = (part[a + reach, lo:hi] + dx0[a] + own_mean).astype(bf16)

    wait(hc)
    hb = gather(n_dp, "dp", d, r * per_row, per_dp, hb_s, hb_r)
    start(hb)
    wait(tc)
    taps_out[...] = scale * jnp.sum(t_col[...], axis=0)
    wait(hb)
    ha = gather(n_row, "row", r, 0, per_row, ha_s, ha_r)
    start(ha)

    for side in range(2):
        @pl.when(sends[side][0])
        def _():
            col_copy(side).wait_send()
            back_copy(side).wait_send()
        @pl.when(row_sends[side][0])
        def _():
            row_copy(side, 0).wait_send()
            for cside in range(2):
                @pl.when(sends[cside][1])
                def _():
                    row_copy(side, 1 + cside).wait_send()
            remote(
                row_send.at[side], row_recv.at[side], pr_s.at[side], pr_r.at[side],
                below if side == 0 else above,
            ).wait_send()

    wait(ha)

    @pl.loop(0, 8)
    def _(m):
        at = pl.ds(pl.multiple_of(m * ch, ch), ch)
        grads_out[at] = final[at].astype(f32) * scale


def x_flat(x_in):
    blocks, depth, ch = x_in.shape
    return x_in[...].reshape(blocks * depth, ch)


def shards(features, cotangent, w_one, w_point, taps, w_pool, w_proj):
    n_dp, n_row, n_col = (lax.axis_size(name) for name in ("dp", "row", "col"))
    total = n_dp * n_row * n_col
    batch, rows, cols, ch = features.shape
    blocks, depth = cols // unit, rows * unit
    wide, tall = blocks + 2 * reach, depth + 2 * edge
    count = rows * cols
    whole = 8 * ch
    per_row = whole // n_row
    per_dp = per_row // n_dp
    per_col = per_dp // n_col

    def split(x):
        x = x.reshape(rows, blocks, unit, ch)
        return jnp.transpose(x, (1, 0, 2, 3)).reshape(blocks, depth, ch)

    def join(x):
        x = x.reshape(blocks, rows, unit, ch)
        return jnp.transpose(x, (1, 0, 2, 3)).reshape(batch, rows, cols, ch)

    vmem = pl.BlockSpec(memory_space=pltpu.VMEM)
    dma = pltpu.SemaphoreType.DMA
    v = pltpu.VMEM
    scratch = [
        v((wide, tall, ch), bf16),
        v((wide, tall, ch), f32),
        v((wide, tall, ch), f32),
        v((4, count, ch), f32),
        v((4, count, ch), bf16),
        v((3, count, ch), bf16),
        v((count, ch), f32),
        v((count, ch), bf16),
        v((4, count, ch), bf16),
        v((3, count, ch), bf16),
        v((blocks, depth, ch), f32),
        v((2, total, 8, ch), f32),
        v((2, 8, ch), f32),
        v((8, ch), f32),
        v((27, 8, ch), f32),
        v((whole, ch), f32),
        v((whole, ch), bf16),
        v((n_row - 1, per_row, ch), bf16),
        v((per_row, ch), bf16),
        v((n_dp - 1, per_dp, ch), bf16),
        v((per_dp, ch), bf16),
        v((n_col - 1, per_col, ch), bf16),
        v((whole, ch), bf16),
        v((n_row, 32, ch), f32),
        v((n_dp, 32, ch), f32),
        v((n_col, 32, ch), f32),
        v((2, wide, edge, ch), bf16),
        v((2, wide, edge, ch), bf16),
        v((2, reach, depth, ch), bf16),
        v((2, reach, depth, ch), bf16),
    ]
    sems = [2, 2, 2, 2, 6, 6, 2, 2, 2, 2]
    sems += [n_row, n_row, n_dp, n_dp, n_col, n_col]
    sems += [n_row, n_row, n_dp, n_dp, n_col, n_col]
    sems += [n_row, n_row, n_dp, n_dp, n_col, n_col]
    scratch += [dma((n,)) for n in sems]
    image_cells = rows * cols * n_row * n_col
    shape = jax.ShapeDtypeStruct
    mixed, dx, grads, g_taps, g_pool, g_four = pl.pallas_call(
        functools.partial(kernel, n_dp, n_row, n_col, image_cells),
        out_shape=(
            shape((blocks, depth, ch), bf16),
            shape((blocks, depth, ch), bf16),
            shape((whole, ch), f32),
            shape((32, ch), f32),
            shape((ch, ch), f32),
            shape((ch, ch), f32),
        ),
        in_specs=[vmem] * 7,
        out_specs=[vmem] * 6,
        scratch_shapes=scratch,
        compiler_params=pltpu.CompilerParams(
            collective_id=0, has_side_effects=True, vmem_limit_bytes=58 << 20
        ),
        cost_estimate=pl.CostEstimate(
            flops=48 * count * ch * ch, bytes_accessed=8 << 20, transcendentals=10 * count * ch
        ),
    )(split(features), split(cotangent), w_one, w_point, taps, w_pool, w_proj)
    return (
        join(mixed),
        join(dx),
        grads[4 * ch : 5 * ch],
        grads[5 * ch :].reshape(3, ch, ch),
        g_taps[:27].reshape(3, 3, 3, ch),
        g_pool,
        jnp.concatenate([grads[: 4 * ch], g_four], axis=0),
    )


def solution(mesh):
    tiled = P("dp", "row", "col", None)
    return jax.shard_map(
        shards,
        mesh=mesh,
        in_specs=(tiled, tiled, P(), P(), P(), P(), P()),
        out_specs=(tiled, tiled, P(), P(), P(), P(), P()),
        check_vma=False,
    )
```

time: 316 us -> 84.9 us (0.27)
  waiting for transfers between devices: 141 us -> 0 us
  Pallas kernels: 0 us -> 71.9 us
  blocking collectives: 70.6 us -> 0 us
  starting transfers between devices: 41.2 us -> 0 us
  other arithmetic: 18.6 us -> 1.14 us
  between operations: 15.6 us -> 0.72 us
  matrix products: 13.3 us -> 0 us
  local copies, waits for them, and re-layouts: 14.3 us -> 10.8 us
    psum x1 -> x0, waiting for transfers between devices: 81.5 us -> none  [shards(): lax.psum((grad_one, grad_point, grad_taps, grad_pool, grad_four), ('dp',...]
    pallas_call x0 -> x1, Pallas kernels: none -> 71.9 us  [shards(): pl.pallas_call(functools.partial(kernel, n_dp, n_row, n_col, image_cells)...]
    psum x2 -> x0, blocking collectives: 70.6 us -> none  [the longest x1 37.8 us: shards(): lax.psum((grad_main, holder), ('dp', 'row', 'col'))]
    ppermute x16 -> x0, waiting for transfers between devices: 59.9 us -> none  [the longest x8 52.5 us: with_halo(): before = lax.ppermute(last, axis, up)]
    ppermute x16 -> x0, starting transfers between devices: 41.1 us -> none  [the longest x8 30.8 us: with_halo(): before = lax.ppermute(last, axis, up)]
    dot_general x19 -> x0, matrix products: 13.3 us -> none  [the longest x5 3.46 us: contract_rows(): lax.dot_general(left_mat, right_mat, (((0,), (0,)), ((), ())), preferred_...]
    convert_element_type x5 -> x0, other arithmetic: 8.33 us -> none  [the longest x1 3.91 us: shards(): grad_input = dx.astype(jnp.bfloat16)]
    mul x9 -> x0, other arithmetic: 5.78 us -> none  [the longest x1 2.17 us: shards(): grad_point * scale]
  transfers between devices with their start and end apart: 17 -> 0, of which waited for: 6 -> 0; matrix products, arithmetic and copies ran while one was open for 4% -> 0% of each run, Pallas kernels for 0% -> 0%
where the time goes in v1:
time: 84.9 us; the launch traced here: 84.6 us
  Pallas kernels  71.9 us (85%)
  local copies, waits for them, and re-layouts  10.8 us (13%)
  other arithmetic  1.14 us (1%)
    pallas_call x1, Pallas kernels, shards(): pl.pallas_call(functools.partial(kernel, n_dp, n_row, n_col, image_cells)...  71.9 us
    unnamed x17, local copies, waits for them, and re-layouts  4.25 us
    slice x1, local copies, waits for them, and re-layouts, shards(): grads[4 * ch:5 * ch]  1.7 us

profile of v1, /device:TPU:0, one launch (start us, length us, event | category | flops | bytes accessed | tf_op | source)
XLA Modules:
  0.0 84.6 jit_solution(10371100014569810419)
XLA Ops:
  0.6 0.0 copy-start.1
  0.6 1.1 %copy.18 = bf16[1,24,24,256]{3,1,2,0:T(8,128)(2,1)S(1)} copy(bf16[1,24,24,256]{3,2,1,0:T(8,128)(2,1)} %param.7) | data formatting | bytes 589824 | tf_op args[0]
  1.7 0.2 copy.19
  1.9 0.7 copy.22.x_in
  2.6 0.0 copy-done.1
  2.6 0.1 copy.20
  2.7 0.2 copy.21
  2.8 0.7 copy.23.cot
  3.6 71.9 %shard_map.126 = (bf16[4,144,256]{2,1,0:T(8,128)(2,1)}, bf16[4,144,256]{2,1,0:T(8,128)(2,1)}, f32[2048,256]{1,0:T(8,128)}, f32[32,256]{1,0:T(8,128)}, f32[256,256]{1,0:T(8,128)}, /*index=5*/f32[256,256]{1,0:T(8,128)}) custom-call(bf16[4,144,256]{2,1,0:T(8,128)(2,1)} %copy.22.x_in, bf16[4,144,256]{2,1,0:T(8,128)(2,1)} %copy.23.cot, bf16[256,256]{1,0:T(8,128)(2,1)} %w_one.1, ...), custom_call_target="tpu_custom_call" | custom-call | flops 1811939328 | bytes 8388608 | tf_op jit(solution)/shard_map/pallas_call | solution.py:523
  75.5 0.0 copy-start.5
  75.5 0.0 copy-start.2
  75.5 1.2 %copy.24 = bf16[4,144,256]{2,0,1:T(4,128)(2,1)S(1)} copy(bf16[4,144,256]{2,1,0:T(8,128)(2,1)} %get-tuple-element.13) | data formatting | bytes 589824 | tf_op jit(solution)/shard_map/pallas_call | solution.py:523
  76.7 0.1 copy.25
  76.7 0.8 copy.28
  77.5 0.0 copy-done.5
  77.5 0.0 copy-start
  77.5 0.6 reshape.53
  78.1 1.7 %slice.12 = f32[256,256]{1,0:T(8,128)} slice(f32[2048,256]{1,0:T(8,128)} %get-tuple-element.15), slice={[1024:1280], [0:256]} | slice | bytes 524288 | tf_op jit(solution)/shard_map/slice | solution.py:546
  79.8 0.0 copy-done.2
  79.8 0.2 copy.26
  80.0 0.1 copy.27
  80.1 0.8 copy.29
  80.8 0.0 copy-done
  80.8 0.9 %slice.13 = f32[768,256]{1,0:T(8,128)} slice(f32[2048,256]{1,0:T(8,128)S(1)} %copy-done), slice={[1280:2048], [0:256]} | slice | bytes 1572864 | tf_op jit(solution)/shard_map/slice | solution.py:547
  81.8 0.0 copy-start.3
  81.8 0.1 slice.15
  81.8 0.9 %copy-done.3 = f32[256,256]{1,0:T(8,128)S(1)} copy-done((f32[256,256]{1,0:T(8,128)S(1)}, f32[256,256]{1,0:T(8,128)}, u32[]{:S(2)}) %copy-start.3) | copy-done | bytes 262168
  82.7 0.0 copy-start.4
  82.7 1.1 %pad_maximum_fusion = f32[1280,256]{1,0:T(8,128)} fusion(f32[256,256]{1,0:T(8,128)S(1)} %copy-done.3, f32[1024,256]{1,0:T(8,128)S(1)} %slice.15), kind=kLoop, calls=%fused_computation | loop fusion | flops 327680 | bytes 2621440 | tf_op jit(solution)/shard_map/concatenate | solution.py:550
  83.8 0.0 copy-done.4
  83.9 0.7 copy.31
Async XLA Ops:
  0.6 2.0 %copy-start.1 = (bf16[1,24,24,256]{3,2,1,0:T(8,128)(2,1)S(1)}, bf16[1,24,24,256]{3,2,1,0:T(8,128)(2,1)}, u32[]{:S(2)}) copy-start(bf16[1,24,24,256]{3,2,1,0:T(8,128)(2,1)} %param.8) | copy-start | bytes 884740
  75.5 2.0 %copy-start.5 = (f32[32,256]{1,0:T(8,128)S(1)}, f32[32,256]{1,0:T(8,128)}, u32[]{:S(2)}) copy-start(f32[32,256]{1,0:T(8,128)} %get-tuple-element.16) | copy-start | bytes 98308
  75.5 4.3 %copy-start.2 = (bf16[4,144,256]{2,1,0:T(8,128)(2,1)S(1)}, bf16[4,144,256]{2,1,0:T(8,128)(2,1)}, u32[]{:S(2)}) copy-start(bf16[4,144,256]{2,1,0:T(8,128)(2,1)} %get-tuple-element.14) | copy-start | bytes 884740
  77.5 3.3 %copy-start = (f32[2048,256]{1,0:T(8,128)S(1)}, f32[2048,256]{1,0:T(8,128)}, u32[]{:S(2)}) copy-start(f32[2048,256]{1,0:T(8,128)} %get-tuple-element.15) | copy-start | bytes 6291460
  81.8 0.9 %copy-start.3 = (f32[256,256]{1,0:T(8,128)S(1)}, f32[256,256]{1,0:T(8,128)}, u32[]{:S(2)}) copy-start(f32[256,256]{1,0:T(8,128)} %get-tuple-element.18) | copy-start | bytes 786436
  82.7 1.1 %copy-start.4 = (f32[256,256]{1,0:T(8,128)S(1)}, f32[256,256]{1,0:T(8,128)}, u32[]{:S(2)}) copy-start(f32[256,256]{1,0:T(8,128)} %get-tuple-element.38) | copy-start | bytes 786436

commit v2 on v1

--- a/solution.py
+++ b/solution.py
@@ -43,6 +43,7 @@
     n_dp, n_row, n_col, image_cells,
     x_in, cot, w_one, w_point, taps, w_pool, w_proj,
     mixed_out, dx_out, grads_out, taps_out, pool_out, four_out,
+    line, flat, tile,
     xp, x32, part, slopes, acts, inner, pre_s, dpre_s, du_s, dz_s, dx0,
     slots, images, term, tapacc,
     g32, gb, g_ra, b1, g_rb, b2, g_rc, final,
@@ -56,7 +57,8 @@
     total = n_dp * n_row * n_col
     per = n_row * n_col
     me = (d * n_row + r) * n_col + c
-    blocks, depth, ch = x_in.shape
+    rows, cols, ch = x_in.shape
+    blocks, depth = cols // unit, rows * unit
     wide = blocks + 2 * reach
     lo, hi = edge, edge + depth
 
@@ -77,11 +79,13 @@
 
     xp[...] = jnp.zeros_like(xp)
     ones = jnp.zeros((8, ch), f32)
+    split(x_in, line, tile)
     for a in range(blocks):
-        block = x_in[a]
-        xp[reach + a, lo:hi] = block
-        ones = ones + fold8(block.astype(f32))
-    slots[0, me] = ones
+        block = tile[a]
+        xp[reach + a, lo:hi] = block.astype(bf16)
+        flat[a * depth : (a + 1) * depth] = block.astype(bf16)
+        ones = ones + fold8(block)
+    slots[0, me] = jnp.sum(ones, axis=0, keepdims=True)
 
     @pl.loop(1, total)
     def _(i):
@@ -135,8 +139,7 @@
     def small_sums(which):
         images[which] = jnp.zeros((8, ch), f32)
         for b in range(n_dp):
-            acc = jnp.sum(slots[which, b * per : (b + 1) * per], axis=0)
-            images[which, b : b + 1] = jnp.sum(acc, axis=0, keepdims=True)
+            images[which, b : b + 1] = jnp.sum(slots[which, b * per : (b + 1) * per], axis=0)
         return images[which]
 
     small_start(0)
@@ -144,7 +147,7 @@
     @pl.loop(0, blocks)
     def _(a):
         here = pl.ds(a * depth, depth)
-        u = dot(x_in[a], w_one[...])
+        u = dot(flat[here], w_one[...])
         act, slope = silu_parts(u)
         act = act.astype(bf16)
         acts[0, here] = act
@@ -156,6 +159,7 @@
         part[a] = jnp.zeros(part.shape[1:], f32)
 
     tapacc[...] = jnp.zeros_like(tapacc)
+    split(cot, line, tile)
 
     for side in range(2):
         @pl.when(sends[side][1])
@@ -209,18 +213,93 @@
     term[...] = jnp.dot(a_four, last, precision=highest, preferred_element_type=f32)
     own_term = term[pl.ds(d, 1), :]
 
-    slots[1, me] = jnp.zeros((8, ch), f32)
+    folded = term
+    folded[...] = jnp.zeros_like(folded)
 
     @pl.loop(0, blocks)
     def _(a):
         here = pl.ds(a * depth, depth)
         out, slope = silu_parts(pre_s[here] + own_term)
-        mixed_out[a] = out.astype(bf16)
-        dpre = (cot[a].astype(f32) * slope).astype(bf16)
+        dpre32 = tile[a] * slope
+        tile[a] = out
+        dpre = dpre32.astype(bf16)
         dpre_s[here] = dpre
-        slots[1, me] += fold8(dpre.astype(f32))
-
+        folded[...] += fold8(dpre.astype(f32))
+
+    slots[1, me] = jnp.sum(folded[...], axis=0, keepdims=True)
     small_start(1)
+
+    half = 4 * ch
+    per_row, per_dp, per_col = (
+        half // n_row,
+        half // (n_row * n_dp),
+        half // (n_row * n_dp * n_col),
+    )
+    bases = (0, r * per_row, r * per_row + d * per_dp, r * per_row + d * per_dp + c * per_col)
+    levels = (
+        ("row", n_row, r, per_row, gb, g_ra, ga_s, ga_r, ha_s, ha_r),
+        ("dp", n_dp, d, per_dp, b1, g_rb, gbs, gbr, hb_s, hb_r),
+        ("col", n_col, c, per_col, b2, g_rc, gc_s, gc_r, hc_s, hc_r),
+    )
+
+    def aligned(x):
+        return pl.multiple_of(x, 16)
+
+    def scatter(h, level):
+        axis, n, at, size, src, dst, ss, rs, _, _ = levels[level]
+        out = []
+        for i in range(1, n):
+            to = lax.rem(at + i, n)
+            out.append(
+                remote(
+                    src.at[h, pl.ds(aligned(to * size), size)], dst.at[h, i - 1],
+                    ss.at[h, i - 1], rs.at[h, i - 1], {axis: to},
+                )
+            )
+        return out
+
+    def add_up(h, level):
+        axis, n, at, size, src, dst = levels[level][:6]
+        step = min(size, 128)
+        out = b1 if level == 0 else b2
+        for p in range(0, size, step):
+            there = pl.ds(aligned(bases[level + 1] + p), step)
+            acc = g32[h, there]
+            for i in range(n - 1):
+                acc = acc + dst[h, i, p : p + step].astype(f32)
+            if level == 2:
+                final[h, there] = acc.astype(bf16)
+            else:
+                g32[h, there] = acc
+                out[h, p : p + step] = acc.astype(bf16)
+
+    def gather(h, level):
+        axis, n, at, size, _, _, _, _, ss, rs = levels[level]
+        own = final.at[h, pl.ds(aligned(bases[level + 1]), size)]
+        return [
+            remote(own, own, ss.at[h, i - 1], rs.at[h, i - 1], {axis: lax.rem(at + i, n)})
+            for i in range(1, n)
+        ]
+
+    def spread(n, axis, at, buf, ss, rs):
+        return [
+            remote(buf.at[at], buf.at[at], ss.at[i - 1], rs.at[i - 1], {axis: lax.rem(at + i, n)})
+            for i in range(1, n)
+        ]
+
+    def start(copies):
+        for copy in copies:
+            copy.start()
+
+    def wait(copies):
+        for copy in copies:
+            copy.wait()
+
+    for m in range(4):
+        g = dot_tn(acts[m], dpre_s[...])
+        g32[0, m * ch : (m + 1) * ch] = g
+        gb[0, m * ch : (m + 1) * ch] = g.astype(bf16)
+    start(scatter(0, 0))
 
     @pl.loop(0, blocks)
     def _(a):
@@ -235,60 +314,16 @@
             else:
                 dz_s[m - 1, here] = dot_nt(du, w_point[m - 1]).astype(bf16)
 
+    wait(scatter(0, 0))
+    add_up(0, 0)
+    start(scatter(0, 1))
     for m in range(4):
-        g = dot_tn(acts[m], dpre_s[...])
-        g32[m * ch : (m + 1) * ch] = g
-        gb[m * ch : (m + 1) * ch] = g.astype(bf16)
-    for m in range(4):
-        g = dot_tn(x_flat(x_in) if m == 0 else inner[m - 1], du_s[m])
-        g32[(4 + m) * ch : (5 + m) * ch] = g
-        gb[(4 + m) * ch : (5 + m) * ch] = g.astype(bf16)
-
-    whole = g32.shape[0]
-    per_row, per_dp, per_col = (
-        whole // n_row,
-        whole // (n_row * n_dp),
-        whole // (n_row * n_dp * n_col),
-    )
-
-    def scatter(n, axis, at, size, src, dst, ss, rs):
-        out = []
-        for i in range(1, n):
-            to = lax.rem(at + i, n)
-            out.append(
-                remote(
-                    src.at[pl.ds(pl.multiple_of(to * size, 16), size)], dst.at[i - 1],
-                    ss.at[i - 1], rs.at[i - 1], {axis: to},
-                )
-            )
-        return out
-
-    def gather(n, axis, at, base, size, ss, rs):
-        own = final.at[pl.ds(pl.multiple_of(base + at * size, 16), size)]
-        return [
-            remote(own, own, ss.at[i - 1], rs.at[i - 1], {axis: lax.rem(at + i, n)})
-            for i in range(1, n)
-        ]
-
-    def spread(n, axis, at, buf, ss, rs):
-        return [
-            remote(buf.at[at], buf.at[at], ss.at[i - 1], rs.at[i - 1], {axis: lax.rem(at + i, n)})
-            for i in range(1, n)
-        ]
-
-    def start(copies):
-        for copy in copies:
-            copy.start()
-
-    def wait(copies):
-        for copy in copies:
-            copy.wait()
-
-    ga = scatter(n_row, "row", r, per_row, gb, g_ra, ga_s, ga_r)
-    start(ga)
-
-    @pl.loop(0, blocks)
-    def _(a):
+        g = dot_tn(flat[...] if m == 0 else inner[m - 1], du_s[m])
+        g32[1, m * ch : (m + 1) * ch] = g
+        gb[1, m * ch : (m + 1) * ch] = g.astype(bf16)
+    start(scatter(1, 0))
+
+    def taps_back(a):
         here = pl.ds(a * depth, depth)
         for k in range(3):
             dz = dz_s[k, here].astype(f32)
@@ -299,6 +334,35 @@
                     tapacc[9 * k + 3 * i + j] += fold8(x32[at, row : row + depth] * dz)
                     part[at, row : row + depth] += dz * taps[k, i, j : j + 1, :]
 
+    middle = blocks // 2
+
+    @pl.loop(0, middle)
+    def _(a):
+        taps_back(a)
+
+    wait(scatter(1, 0))
+    add_up(1, 0)
+    wait(scatter(0, 1))
+    add_up(0, 1)
+    start(scatter(0, 2))
+    start(scatter(1, 1))
+
+    @pl.loop(middle, blocks)
+    def _(a):
+        taps_back(a)
+
+    def edge_copy(side):
+        return remote(
+            row_send.at[side], row_recv.at[side], pr_s.at[side], pr_r.at[side],
+            below if side == 0 else above,
+        )
+
+    def back_copy(side):
+        return remote(
+            col_send.at[side], col_recv.at[side], pc_s.at[side], pc_r.at[side],
+            right if side == 0 else left,
+        )
+
     for side in range(2):
         @pl.when(row_sends[side][0])
         def _():
@@ -306,21 +370,11 @@
             @pl.loop(0, wide)
             def _(a):
                 row_send[side, a] = part[a, src : src + edge].astype(bf16)
-            remote(
-                row_send.at[side], row_recv.at[side], pr_s.at[side], pr_r.at[side],
-                below if side == 0 else above,
-            ).start()
-
-    wait(ga)
-    mine = pl.multiple_of(r * per_row, 16)
-    for s in range(0, per_row, 128):
-        acc = g32[pl.ds(pl.multiple_of(mine + s, 16), 128)]
-        for i in range(n_row - 1):
-            acc = acc + g_ra[i, s : s + 128].astype(f32)
-        g32[pl.ds(pl.multiple_of(mine + s, 16), 128)] = acc
-        b1[s : s + 128] = acc.astype(bf16)
-    gbc = scatter(n_dp, "dp", d, per_dp, b1, g_rb, gbs, gbr)
-    start(gbc)
+            edge_copy(side).start()
+
+    wait(scatter(0, 2))
+    add_up(0, 2)
+    start(gather(0, 2))
 
     t_row[r] = jnp.zeros(t_row.shape[1:], f32)
     for t in range(27):
@@ -331,21 +385,12 @@
     for side in range(2):
         @pl.when(row_sends[side][1])
         def _():
-            remote(
-                row_send.at[side], row_recv.at[side], pr_s.at[side], pr_r.at[side],
-                below if side == 0 else above,
-            ).wait_recv()
+            edge_copy(side).wait_recv()
             dst = lo if side == 0 else hi - edge
             @pl.loop(0, wide)
             def _(a):
                 part[a, dst : dst + edge] += row_recv[side, a].astype(f32)
 
-    def back_copy(side):
-        return remote(
-            col_send.at[side], col_recv.at[side], pc_s.at[side], pc_r.at[side],
-            right if side == 0 else left,
-        )
-
     for side in range(2):
         @pl.when(sends[side][0])
         def _():
@@ -354,26 +399,16 @@
                 col_send[side, a] = part[src + a, lo:hi].astype(bf16)
             back_copy(side).start()
 
+    wait(scatter(1, 1))
+    add_up(1, 1)
+    start(scatter(1, 2))
+
     wait(ta)
     t_dp[d] = jnp.sum(t_row[...], axis=0)
     tb = spread(n_dp, "dp", d, t_dp, tb_s, tb_r)
     start(tb)
 
-    wait(gbc)
-    mine = pl.multiple_of(mine + d * per_dp, 16)
-    for s in range(0, per_dp, 64):
-        acc = g32[pl.ds(pl.multiple_of(mine + s, 16), 64)]
-        for i in range(n_dp - 1):
-            acc = acc + g_rb[i, s : s + 64].astype(f32)
-        g32[pl.ds(pl.multiple_of(mine + s, 16), 64)] = acc
-        b2[s : s + 64] = acc.astype(bf16)
-    gc = scatter(n_col, "col", c, per_col, b2, g_rc, gc_s, gc_r)
-    start(gc)
-
-    wait(tb)
-    t_col[c] = jnp.sum(t_dp[...], axis=0)
-    tc = spread(n_col, "col", c, t_col, tc_s, tc_r)
-    start(tc)
+    join(tile, line, mixed_out)
 
     small_wait(1)
     slope_total = small_sums(1)
@@ -398,14 +433,18 @@
         preferred_element_type=f32,
     )
 
-    wait(gc)
-    mine = pl.multiple_of(mine + c * per_col, 16)
-    acc = g32[pl.ds(mine, per_col)]
-    for i in range(n_col - 1):
-        acc = acc + g_rc[i].astype(f32)
-    final[pl.ds(mine, per_col)] = acc.astype(bf16)
-    hc = gather(n_col, "col", c, r * per_row + d * per_dp, per_col, hc_s, hc_r)
-    start(hc)
+    wait(gather(0, 2))
+    start(gather(0, 1))
+    wait(tb)
+    t_col[c] = jnp.sum(t_dp[...], axis=0)
+    tc = spread(n_col, "col", c, t_col, tc_s, tc_r)
+    start(tc)
+
+    wait(scatter(1, 2))
+    add_up(1, 2)
+    start(gather(1, 2))
+    wait(gather(0, 1))
+    start(gather(0, 0))
 
     for side in range(2):
         @pl.when(sends[side][1])
@@ -415,24 +454,27 @@
             for a in range(reach):
                 part[dst + a, lo:hi] += col_recv[side, a].astype(f32)
 
+    wait(gather(1, 2))
+    start(gather(1, 1))
+
     @pl.loop(0, blocks)
     def _(a):
-        dx_out[a] = (part[a + reach, lo:hi] + dx0[a] + own_mean).astype(bf16)
-
-    wait(hc)
-    hb = gather(n_dp, "dp", d, r * per_row, per_dp, hb_s, hb_r)
-    start(hb)
+        tile[a] = part[a + reach, lo:hi] + dx0[a] + own_mean
+
+    join(tile, line, dx_out)
     wait(tc)
     taps_out[...] = scale * jnp.sum(t_col[...], axis=0)
-    wait(hb)
-    ha = gather(n_row, "row", r, 0, per_row, ha_s, ha_r)
-    start(ha)
+    wait(gather(0, 0))
+    grads_out[0:half] = final[0]
+    wait(gather(1, 1))
+    start(gather(1, 0))
 
     for side in range(2):
         @pl.when(sends[side][0])
         def _():
             col_copy(side).wait_send()
             back_copy(side).wait_send()
+
         @pl.when(row_sends[side][0])
         def _():
             row_copy(side, 0).wait_send()
@@ -440,22 +482,53 @@
                 @pl.when(sends[cside][1])
                 def _():
                     row_copy(side, 1 + cside).wait_send()
-            remote(
-                row_send.at[side], row_recv.at[side], pr_s.at[side], pr_r.at[side],
-                below if side == 0 else above,
-            ).wait_send()
-
-    wait(ha)
-
-    @pl.loop(0, 8)
-    def _(m):
-        at = pl.ds(pl.multiple_of(m * ch, ch), ch)
-        grads_out[at] = final[at].astype(f32) * scale
-
-
-def x_flat(x_in):
-    blocks, depth, ch = x_in.shape
-    return x_in[...].reshape(blocks * depth, ch)
+            edge_copy(side).wait_send()
+
+    wait(gather(1, 0))
+    grads_out[half : 2 * half] = final[1]
+
+
+def split(src, line, tile):
+    rows, cols, _ = src.shape
+    for p in range(rows):
+        line[p % 2] = src[p].astype(f32)
+        for a in range(cols // unit):
+            tile[a, unit * p : unit * (p + 1)] = line[p % 2, unit * a : unit * (a + 1)]
+
+
+def join(tile, line, dst):
+    rows, cols, _ = dst.shape
+    for p in range(rows):
+        for a in range(cols // unit):
+            line[p % 2, unit * a : unit * (a + 1)] = tile[a, unit * p : unit * (p + 1)]
+        dst[p] = line[p % 2].astype(bf16)
+
+
+def finish(
+    scale, grads, g_taps, pool, four, mixed_in, dx_in,
+    one, point, taps, pool_out, proj, mixed_out, dx_out, sems,
+):
+    ch = pool.shape[0]
+    moves = (
+        pltpu.make_async_copy(mixed_in, mixed_out, sems.at[0]),
+        pltpu.make_async_copy(dx_in, dx_out, sems.at[1]),
+        pltpu.make_async_copy(pool, pool_out, sems.at[2]),
+    )
+    for move in moves:
+        move.start()
+    proj[4 * ch : 5 * ch] = four[...]
+    for m in range(8):
+        block = grads[m * ch : (m + 1) * ch].astype(f32) * scale
+        if m < 4:
+            proj[m * ch : (m + 1) * ch] = block
+        elif m == 4:
+            one[...] = block
+        else:
+            point[m - 5] = block
+    for t in range(27):
+        taps[t // 9, t // 3 % 3, t % 3 : t % 3 + 1, :] = g_taps[t : t + 1, :]
+    for move in moves:
+        move.wait()
 
 
 def shards(features, cotangent, w_one, w_point, taps, w_pool, w_proj):
@@ -465,23 +538,18 @@
     blocks, depth = cols // unit, rows * unit
     wide, tall = blocks + 2 * reach, depth + 2 * edge
     count = rows * cols
-    whole = 8 * ch
-    per_row = whole // n_row
+    half = 4 * ch
+    per_row = half // n_row
     per_dp = per_row // n_dp
     per_col = per_dp // n_col
-
-    def split(x):
-        x = x.reshape(rows, blocks, unit, ch)
-        return jnp.transpose(x, (1, 0, 2, 3)).reshape(blocks, depth, ch)
-
-    def join(x):
-        x = x.reshape(blocks, rows, unit, ch)
-        return jnp.transpose(x, (1, 0, 2, 3)).reshape(batch, rows, cols, ch)
 
     vmem = pl.BlockSpec(memory_space=pltpu.VMEM)
     dma = pltpu.SemaphoreType.DMA
     v = pltpu.VMEM
     scratch = [
+        v((2, cols, ch), f32),
+        v((count, ch), bf16),
+        v((blocks, depth, ch), f32),
         v((wide, tall, ch), bf16),
         v((wide, tall, ch), f32),
         v((wide, tall, ch), f32),
@@ -493,18 +561,18 @@
         v((4, count, ch), bf16),
         v((3, count, ch), bf16),
         v((blocks, depth, ch), f32),
-        v((2, total, 8, ch), f32),
+        v((2, total, 1, ch), f32),
         v((2, 8, ch), f32),
         v((8, ch), f32),
         v((27, 8, ch), f32),
-        v((whole, ch), f32),
-        v((whole, ch), bf16),
-        v((n_row - 1, per_row, ch), bf16),
-        v((per_row, ch), bf16),
-        v((n_dp - 1, per_dp, ch), bf16),
-        v((per_dp, ch), bf16),
-        v((n_col - 1, per_col, ch), bf16),
-        v((whole, ch), bf16),
+        v((2, half, ch), f32),
+        v((2, half, ch), bf16),
+        v((2, n_row - 1, per_row, ch), bf16),
+        v((2, per_row, ch), bf16),
+        v((2, n_dp - 1, per_dp, ch), bf16),
+        v((2, per_dp, ch), bf16),
+        v((2, n_col - 1, per_col, ch), bf16),
+        v((2, half, ch), bf16),
         v((n_row, 32, ch), f32),
         v((n_dp, 32, ch), f32),
         v((n_col, 32, ch), f32),
@@ -513,19 +581,18 @@
         v((2, reach, depth, ch), bf16),
         v((2, reach, depth, ch), bf16),
     ]
-    sems = [2, 2, 2, 2, 6, 6, 2, 2, 2, 2]
-    sems += [n_row, n_row, n_dp, n_dp, n_col, n_col]
-    sems += [n_row, n_row, n_dp, n_dp, n_col, n_col]
-    sems += [n_row, n_row, n_dp, n_dp, n_col, n_col]
-    scratch += [dma((n,)) for n in sems]
+    levels = [n_row, n_row, n_dp, n_dp, n_col, n_col]
+    sems = [(n,) for n in (2, 2, 2, 2, 6, 6, 2, 2, 2, 2)]
+    sems += [(2, n) for n in levels] * 2 + [(n,) for n in levels]
+    scratch += [dma(n) for n in sems]
     image_cells = rows * cols * n_row * n_col
     shape = jax.ShapeDtypeStruct
     mixed, dx, grads, g_taps, g_pool, g_four = pl.pallas_call(
         functools.partial(kernel, n_dp, n_row, n_col, image_cells),
         out_shape=(
-            shape((blocks, depth, ch), bf16),
-            shape((blocks, depth, ch), bf16),
-            shape((whole, ch), f32),
+            shape((rows, cols, ch), bf16),
+            shape((rows, cols, ch), bf16),
+            shape((2 * half, ch), bf16),
             shape((32, ch), f32),
             shape((ch, ch), f32),
             shape((ch, ch), f32),
@@ -539,16 +606,31 @@
         cost_estimate=pl.CostEstimate(
             flops=48 * count * ch * ch, bytes_accessed=8 << 20, transcendentals=10 * count * ch
         ),
-    )(split(features), split(cotangent), w_one, w_point, taps, w_pool, w_proj)
-    return (
-        join(mixed),
-        join(dx),
-        grads[4 * ch : 5 * ch],
-        grads[5 * ch :].reshape(3, ch, ch),
-        g_taps[:27].reshape(3, 3, 3, ch),
-        g_pool,
-        jnp.concatenate([grads[: 4 * ch], g_four], axis=0),
-    )
+    )(
+        features.reshape(rows, cols, ch), cotangent.reshape(rows, cols, ch),
+        w_one, w_point, taps, w_pool, w_proj,
+    )
+    scale = 1.0 / math.sqrt(image_cells * n_dp)
+    hbm = pl.BlockSpec(memory_space=pl.ANY)
+    one, point, taps_out, pool, proj, mixed, dx = pl.pallas_call(
+        functools.partial(finish, scale),
+        out_shape=(
+            shape((ch, ch), f32),
+            shape((3, ch, ch), f32),
+            shape((3, 3, 3, ch), f32),
+            shape((ch, ch), f32),
+            shape((5 * ch, ch), f32),
+            shape((rows, cols, ch), bf16),
+            shape((rows, cols, ch), bf16),
+        ),
+        in_specs=[vmem, vmem, hbm, vmem, hbm, hbm],
+        out_specs=[vmem, vmem, vmem, hbm, vmem, hbm, hbm],
+        scratch_shapes=[dma((3,))],
+        compiler_params=pltpu.CompilerParams(vmem_limit_bytes=24 << 20),
+        cost_estimate=pl.CostEstimate(flops=0, bytes_accessed=8 << 20, transcendentals=0),
+    )(grads, g_taps, g_pool, g_four, mixed, dx)
+    tiled = (batch, rows, cols, ch)
+    return (mixed.reshape(tiled), dx.reshape(tiled), one, point, taps_out, pool, proj)
 
 
 def solution(mesh):

time: 84.9 us -> 76 us (0.90)
  local copies, waits for them, and re-layouts: 10.8 us -> 5.8 us
  Pallas kernels: 71.9 us -> 69.1 us
  other arithmetic: 1.14 us -> 0 us
    pallas_call x1, Pallas kernels: 71.9 us -> 66.8 us  [shards(): pl.pallas_call(functools.partial(kernel, n_dp, n_row, n_col, image_cells)...]
    slice x3 -> x0, local copies, waits for them, and re-layouts: 2.7 us -> none  [the longest x1 1.7 us: shards(): grads[4 * ch:5 * ch]]
    pallas_call x0 -> x1, Pallas kernels: none -> 2.33 us  [shards(): pl.pallas_call(functools.partial(finish, scale), out_shape=(shape((ch, ch...]
    reshape x3 -> x0, local copies, waits for them, and re-layouts: 2.12 us -> none  [the longest x2 1.49 us: split(): return jnp.transpose(x, (1, 0, 2, 3)).reshape(blocks, depth, ch)]
    unnamed x17 -> x12, local copies, waits for them, and re-layouts: 4.25 us -> 5.8 us
    pallas_call x2 -> x0, local copies, waits for them, and re-layouts: 1.31 us -> none  [shards(): pl.pallas_call(functools.partial(kernel, n_dp, n_row, n_col, image_cells)...]
    concatenate x1 -> x0, other arithmetic: 1.14 us -> none  [shards(): jnp.concatenate([grads[:4 * ch], g_four], axis=0)]
where the time goes in v2:
time: 76 us; the launch traced here: 75.6 us
  Pallas kernels  69.1 us (91%)
  local copies, waits for them, and re-layouts  5.8 us (8%)
    pallas_call x1, Pallas kernels, shards(): pl.pallas_call(functools.partial(kernel, n_dp, n_row, n_col, image_cells)...  66.8 us
    unnamed x12, local copies, waits for them, and re-layouts  5.8 us
    pallas_call x1, Pallas kernels, shards(): pl.pallas_call(functools.partial(finish, scale), out_shape=(shape((ch, ch...  2.33 us

profile of v2, /device:TPU:0, one launch (start us, length us, event | category | flops | bytes accessed | tf_op | source)
XLA Modules:
  0.0 75.6 jit_solution(12977971778153307003)
XLA Ops:
  0.6 66.8 %shard_map.126 = (bf16[24,24,256]{2,1,0:T(8,128)(2,1)}, bf16[24,24,256]{2,1,0:T(8,128)(2,1)}, bf16[2048,256]{1,0:T(8,128)(2,1)}, f32[32,256]{1,0:T(8,128)}, f32[256,256]{1,0:T(8,128)}, /*index=5*/f32[256,256]{1,0:T(8,128)}) custom-call(bf16[24,24,256]{2,1,0:T(8,128)(2,1)} %bitcast.4, bf16[24,24,256]{2,1,0:T(8,128)(2,1)} %bitcast.5, bf16[256,256]{1,0:T(8,128)(2,1)} %w_one.1, ...), custom_call_target="tpu_custom_call" | custom-call | flops 1811939328 | bytes 8388608 | tf_op jit(solution)/shard_map/pallas_call | solution.py:590
  67.4 0.0 copy-start
  67.4 1.2 %copy-done = bf16[2048,256]{1,0:T(8,128)(2,1)S(1)} copy-done((bf16[2048,256]{1,0:T(8,128)(2,1)S(1)}, bf16[2048,256]{1,0:T(8,128)(2,1)}, u32[]{:S(2)}) %copy-start) | copy-done | bytes 1048600
  68.6 0.0 copy-start.1
  68.7 1.0 %copy-done.1 = bf16[24,24,256]{2,1,0:T(8,128)(2,1)S(1)} copy-done((bf16[24,24,256]{2,1,0:T(8,128)(2,1)S(1)}, bf16[24,24,256]{2,1,0:T(8,128)(2,1)}, u32[]{:S(2)}) %copy-start.1) | copy-done | bytes 294936
  69.6 0.0 copy-start.2
  69.6 1.0 %copy-done.2 = bf16[24,24,256]{2,1,0:T(8,128)(2,1)S(1)} copy-done((bf16[24,24,256]{2,1,0:T(8,128)(2,1)S(1)}, bf16[24,24,256]{2,1,0:T(8,128)(2,1)}, u32[]{:S(2)}) %copy-start.2) | copy-done | bytes 294936
  70.6 0.0 copy-start.3
  70.6 0.9 %copy-done.3 = f32[256,256]{1,0:T(8,128)S(1)} copy-done((f32[256,256]{1,0:T(8,128)S(1)}, f32[256,256]{1,0:T(8,128)}, u32[]{:S(2)}) %copy-start.3) | copy-done | bytes 262168
  71.5 0.0 copy-start.4
  71.5 0.9 %copy-done.4 = f32[256,256]{1,0:T(8,128)S(1)} copy-done((f32[256,256]{1,0:T(8,128)S(1)}, f32[256,256]{1,0:T(8,128)}, u32[]{:S(2)}) %copy-start.4) | copy-done | bytes 262168
  72.5 0.0 copy-start.5
  72.5 0.8 %copy-done.5 = f32[32,256]{1,0:T(8,128)S(1)} copy-done((f32[32,256]{1,0:T(8,128)S(1)}, f32[32,256]{1,0:T(8,128)}, u32[]{:S(2)}) %copy-start.5) | copy-done | bytes 32792
  73.2 2.3 %shard_map.127 = (f32[256,256]{1,0:T(8,128)}, f32[3,256,256]{2,1,0:T(8,128)}, f32[3,3,3,256]{3,2,1,0:T(4,128)}, f32[256,256]{1,0:T(8,128)}, f32[1280,256]{1,0:T(...) custom-call(bf16[2048,256]{1,0:T(8,128)(2,1)S(1)} %copy-done, f32[32,256]{1,0:T(8,128)S(1)} %copy-done.5, ...), custom_call_target="tpu_custom_call" | custom-call | bytes 8388608 | tf_op jit(solution)/shard_map/pallas_call | solution.py:615
Async XLA Ops:
  67.4 1.2 %copy-start = (bf16[2048,256]{1,0:T(8,128)(2,1)S(1)}, bf16[2048,256]{1,0:T(8,128)(2,1)}, u32[]{:S(2)}) copy-start(bf16[2048,256]{1,0:T(8,128)(2,1)} %get-tuple-element.20.grads) | copy-start | bytes 3145732
  68.6 1.0 %copy-start.1 = (bf16[24,24,256]{2,1,0:T(8,128)(2,1)S(1)}, bf16[24,24,256]{2,1,0:T(8,128)(2,1)}, u32[]{:S(2)}) copy-start(bf16[24,24,256]{2,1,0:T(8,128)(2,1)} %get-tuple-element.24.mixed_in) | copy-start | bytes 884740
  69.6 1.0 %copy-start.2 = (bf16[24,24,256]{2,1,0:T(8,128)(2,1)S(1)}, bf16[24,24,256]{2,1,0:T(8,128)(2,1)}, u32[]{:S(2)}) copy-start(bf16[24,24,256]{2,1,0:T(8,128)(2,1)} %get-tuple-element.25.dx_in) | copy-start | bytes 884740
  70.6 0.9 %copy-start.3 = (f32[256,256]{1,0:T(8,128)S(1)}, f32[256,256]{1,0:T(8,128)}, u32[]{:S(2)}) copy-start(f32[256,256]{1,0:T(8,128)} %get-tuple-element.22.pool) | copy-start | bytes 786436
  71.5 0.9 %copy-start.4 = (f32[256,256]{1,0:T(8,128)S(1)}, f32[256,256]{1,0:T(8,128)}, u32[]{:S(2)}) copy-start(f32[256,256]{1,0:T(8,128)} %get-tuple-element.23.four) | copy-start | bytes 786436
  72.5 0.8 %copy-start.5 = (f32[32,256]{1,0:T(8,128)S(1)}, f32[32,256]{1,0:T(8,128)}, u32[]{:S(2)}) copy-start(f32[32,256]{1,0:T(8,128)} %get-tuple-element.21.g_taps) | copy-start | bytes 98308

commit v3 on v2

--- a/solution.py
+++ b/solution.py
@@ -45,30 +45,20 @@
     mixed_out, dx_out, grads_out, taps_out, pool_out, four_out,
     line, flat, tile,
     xp, x32, part, slopes, acts, inner, pre_s, dpre_s, du_s, dz_s, dx0,
-    slots, images, term, tapacc,
+    s_row, s_col, s_dp, images, term, tapacc,
     g32, gb, g_ra, b1, g_rb, b2, g_rc, final,
     t_row, t_dp, t_col,
     row_send, row_recv, col_send, col_recv,
-    sm_s, sm_r, xc_s, xc_r, xr_s, xr_r, pr_s, pr_r, pc_s, pc_r,
+    xc_s, xc_r, xr_s, xr_r, pr_s, pr_r, pc_s, pc_r,
     ga_s, ga_r, gbs, gbr, gc_s, gc_r, ha_s, ha_r, hb_s, hb_r, hc_s, hc_r,
     ta_s, ta_r, tb_s, tb_r, tc_s, tc_r,
+    sa_s, sa_r, sb_s, sb_r, sc_s, sc_r,
 ):
     d, r, c = lax.axis_index("dp"), lax.axis_index("row"), lax.axis_index("col")
-    total = n_dp * n_row * n_col
-    per = n_row * n_col
-    me = (d * n_row + r) * n_col + c
     rows, cols, ch = x_in.shape
     blocks, depth = cols // unit, rows * unit
     wide = blocks + 2 * reach
     lo, hi = edge, edge + depth
-
-    def peer(i):
-        p = lax.rem(me + i, total)
-        return {
-            "dp": lax.div(p, per),
-            "row": lax.rem(lax.div(p, n_col), n_row),
-            "col": lax.rem(p, n_col),
-        }
 
     def remote(src, dst, ss, rs, dev):
         return pltpu.make_async_remote_copy(
@@ -85,13 +75,15 @@
         xp[reach + a, lo:hi] = block.astype(bf16)
         flat[a * depth : (a + 1) * depth] = block.astype(bf16)
         ones = ones + fold8(block)
-    slots[0, me] = jnp.sum(ones, axis=0, keepdims=True)
-
-    @pl.loop(1, total)
-    def _(i):
-        pl.semaphore_signal(barrier, inc=1, device_id=peer(i), device_id_type=MESH)
-
-    pl.semaphore_wait(barrier, total - 1)
+    s_row[0, r] = jnp.sum(ones, axis=0, keepdims=True)
+
+    for axis, n, at in (("col", n_col, c), ("row", n_row, r), ("dp", n_dp, d)):
+        for i in range(1, n):
+            pl.semaphore_signal(
+                barrier, inc=1, device_id={axis: lax.rem(at + i, n)}, device_id_type=MESH
+            )
+
+    pl.semaphore_wait(barrier, n_col + n_row + n_dp - 3)
 
     right, left = {"col": lax.rem(c + 1, n_col)}, {"col": lax.rem(c + n_col - 1, n_col)}
     below, above = {"row": lax.rem(r + 1, n_row)}, {"row": lax.rem(r + n_row - 1, n_row)}
@@ -125,24 +117,44 @@
         def _():
             row_copy(side, 0).start()
 
-    def small_start(which):
-        @pl.loop(1, total)
-        def _(i):
-            remote(
-                slots.at[which, me], slots.at[which, me], sm_s.at[which], sm_r.at[which], peer(i)
-            ).start()
-
-    def small_wait(which):
-        rest = slots.at[which, pl.ds(0, total - 1)]
-        remote(rest, rest, sm_s.at[which], sm_r.at[which], peer(1)).wait()
+    def spread(n, axis, at, buf, ss, rs, pre=()):
+        own = buf.at[(*pre, at)]
+        return [
+            remote(own, own, ss.at[(*pre, i - 1)], rs.at[(*pre, i - 1)], {axis: lax.rem(at + i, n)})
+            for i in range(1, n)
+        ]
+
+    def start(copies):
+        for copy in copies:
+            copy.start()
+
+    def wait(copies):
+        for copy in copies:
+            copy.wait()
+
+    def small(level, which):
+        if level == 0:
+            return spread(n_row, "row", r, s_row, sa_s, sa_r, (which,))
+        if level == 1:
+            return spread(n_col, "col", c, s_col, sc_s, sc_r, (which,))
+        return spread(n_dp, "dp", d, s_dp, sb_s, sb_r, (which,))
+
+    def small_next(level, which):
+        wait(small(level, which))
+        if level == 0:
+            s_col[which, c] = jnp.sum(s_row[which], axis=0)
+        else:
+            s_dp[which, d] = jnp.sum(s_col[which], axis=0)
+        start(small(level + 1, which))
 
     def small_sums(which):
+        wait(small(2, which))
         images[which] = jnp.zeros((8, ch), f32)
         for b in range(n_dp):
-            images[which, b : b + 1] = jnp.sum(slots[which, b * per : (b + 1) * per], axis=0)
+            images[which, b : b + 1] = s_dp[which, b]
         return images[which]
 
-    small_start(0)
+    start(small(0, 0))
 
     @pl.loop(0, blocks)
     def _(a):
@@ -154,12 +166,15 @@
         slopes[0, here] = slope
         pre_s[here] = dot(act, w_proj[0:ch])
 
+    small_next(0, 0)
+
     @pl.loop(0, wide)
     def _(a):
         part[a] = jnp.zeros(part.shape[1:], f32)
 
     tapacc[...] = jnp.zeros_like(tapacc)
     split(cot, line, tile)
+    small_next(1, 0)
 
     for side in range(2):
         @pl.when(sends[side][1])
@@ -204,7 +219,6 @@
             pre = pre + dot(act, w_proj[(k + 1) * ch : (k + 2) * ch])
         pre_s[here] = pre
 
-    small_wait(0)
     pooled = small_sums(0) * (1.0 / image_cells)
     pool32 = w_pool[...].astype(f32)
     last = w_proj[4 * ch : 5 * ch].astype(f32)
@@ -226,8 +240,8 @@
         dpre_s[here] = dpre
         folded[...] += fold8(dpre.astype(f32))
 
-    slots[1, me] = jnp.sum(folded[...], axis=0, keepdims=True)
-    small_start(1)
+    s_row[1, r] = jnp.sum(folded[...], axis=0, keepdims=True)
+    start(small(0, 1))
 
     half = 4 * ch
     per_row, per_dp, per_col = (
@@ -281,20 +295,6 @@
             for i in range(1, n)
         ]
 
-    def spread(n, axis, at, buf, ss, rs):
-        return [
-            remote(buf.at[at], buf.at[at], ss.at[i - 1], rs.at[i - 1], {axis: lax.rem(at + i, n)})
-            for i in range(1, n)
-        ]
-
-    def start(copies):
-        for copy in copies:
-            copy.start()
-
-    def wait(copies):
-        for copy in copies:
-            copy.wait()
-
     for m in range(4):
         g = dot_tn(acts[m], dpre_s[...])
         g32[0, m * ch : (m + 1) * ch] = g
@@ -314,6 +314,7 @@
             else:
                 dz_s[m - 1, here] = dot_nt(du, w_point[m - 1]).astype(bf16)
 
+    small_next(0, 1)
     wait(scatter(0, 0))
     add_up(0, 0)
     start(scatter(0, 1))
@@ -340,6 +341,7 @@
     def _(a):
         taps_back(a)
 
+    small_next(1, 1)
     wait(scatter(1, 0))
     add_up(1, 0)
     wait(scatter(0, 1))
@@ -410,7 +412,6 @@
 
     join(tile, line, mixed_out)
 
-    small_wait(1)
     slope_total = small_sums(1)
     dq = (
         lax.dot_general(
@@ -533,7 +534,6 @@
 
 def shards(features, cotangent, w_one, w_point, taps, w_pool, w_proj):
     n_dp, n_row, n_col = (lax.axis_size(name) for name in ("dp", "row", "col"))
-    total = n_dp * n_row * n_col
     batch, rows, cols, ch = features.shape
     blocks, depth = cols // unit, rows * unit
     wide, tall = blocks + 2 * reach, depth + 2 * edge
@@ -561,7 +561,9 @@
         v((4, count, ch), bf16),
         v((3, count, ch), bf16),
         v((blocks, depth, ch), f32),
-        v((2, total, 1, ch), f32),
+        v((2, n_row, 1, ch), f32),
+        v((2, n_col, 1, ch), f32),
+        v((2, n_dp, 1, ch), f32),
         v((2, 8, ch), f32),
         v((8, ch), f32),
         v((27, 8, ch), f32),
@@ -582,8 +584,8 @@
         v((2, reach, depth, ch), bf16),
     ]
     levels = [n_row, n_row, n_dp, n_dp, n_col, n_col]
-    sems = [(n,) for n in (2, 2, 2, 2, 6, 6, 2, 2, 2, 2)]
-    sems += [(2, n) for n in levels] * 2 + [(n,) for n in levels]
+    sems = [(n,) for n in (2, 2, 6, 6, 2, 2, 2, 2)]
+    sems += [(2, n) for n in levels] * 2 + [(n,) for n in levels] + [(2, n) for n in levels]
     scratch += [dma(n) for n in sems]
     image_cells = rows * cols * n_row * n_col
     shape = jax.ShapeDtypeStruct
@@ -626,7 +628,7 @@
         in_specs=[vmem, vmem, hbm, vmem, hbm, hbm],
         out_specs=[vmem, vmem, vmem, hbm, vmem, hbm, hbm],
         scratch_shapes=[dma((3,))],
-        compiler_params=pltpu.CompilerParams(vmem_limit_bytes=24 << 20),
+        compiler_params=pltpu.CompilerParams(vmem_limit_bytes=58 << 20),
         cost_estimate=pl.CostEstimate(flops=0, bytes_accessed=8 << 20, transcendentals=0),
     )(grads, g_taps, g_pool, g_four, mixed, dx)
     tiled = (batch, rows, cols, ch)

time: 76 us -> 94.7 us (1.25)
  Pallas kernels: 69.1 us -> 93.9 us
  local copies, waits for them, and re-layouts: 5.8 us -> 0 us
    pallas_call x1, Pallas kernels: 2.33 us -> 29.6 us  [shards(): pl.pallas_call(functools.partial(finish, scale), out_shape=(shape((ch, ch...]
    unnamed x12 -> x0, local copies, waits for them, and re-layouts: 5.8 us -> none
    pallas_call x1, Pallas kernels: 66.8 us -> 64.3 us  [shards(): pl.pallas_call(functools.partial(kernel, n_dp, n_row, n_col, image_cells)...]
where the time goes in v3:
time: 94.7 us; the launch traced here: 94.6 us
  Pallas kernels  93.9 us (99%)
    pallas_call x1, Pallas kernels, shards(): pl.pallas_call(functools.partial(kernel, n_dp, n_row, n_col, image_cells)...  64.3 us
    pallas_call x1, Pallas kernels, shards(): pl.pallas_call(functools.partial(finish, scale), out_shape=(shape((ch, ch...  29.6 us

profile of v3, /device:TPU:0, one launch (start us, length us, event | category | flops | bytes accessed | tf_op | source)
XLA Modules:
  0.0 94.6 jit_solution(5098009445368577740)
XLA Ops:
  0.6 64.3 %shard_map.126 = (bf16[24,24,256]{2,1,0:T(8,128)(2,1)}, bf16[24,24,256]{2,1,0:T(8,128)(2,1)}, bf16[2048,256]{1,0:T(8,128)(2,1)}, f32[32,256]{1,0:T(8,128)}, f32[256,256]{1,0:T(8,128)}, /*index=5*/f32[256,256]{1,0:T(8,128)}) custom-call(bf16[24,24,256]{2,1,0:T(8,128)(2,1)} %bitcast.4, bf16[24,24,256]{2,1,0:T(8,128)(2,1)} %bitcast.5, bf16[256,256]{1,0:T(8,128)(2,1)} %w_one.1, ...), custom_call_target="tpu_custom_call" | custom-call | flops 1811939328 | bytes 8388608 | tf_op jit(solution)/shard_map/pallas_call | solution.py:592
  64.9 29.6 %shard_map.127 = (f32[256,256]{1,0:T(8,128)}, f32[3,256,256]{2,1,0:T(8,128)}, f32[3,3,3,256]{3,2,1,0:T(4,128)}, f32[256,256]{1,0:T(8,128)}, f32[1280,256]{1,0:T(...) custom-call(bf16[2048,256]{1,0:T(8,128)(2,1)} %get-tuple-element.20.grads, ...), custom_call_target="tpu_custom_call" | custom-call | bytes 8388608 | tf_op jit(solution)/shard_map/pallas_call | solution.py:617
